TPU v7x, 32 devices: a whole 2x2x4 slice. The times are simulated.
32 devices in a mesh: dp: 2 (over y), mp: 16 (over z, x, core).
Axes of the slice: x: 2, y: 2, z: 4, core: 2. Of those that a mesh axis runs over, the one named last changes fastest.
Arguments:
- dec_input: bfloat16 [2, 256, 4096], P('dp', None, 'mp'), may hold values from -6 to 6
- enc_output: bfloat16 [2, 256, 4096], P('dp', 'mp'), may hold values from -32 to 32
- query_weight: bfloat16 [4096, 4096], P('dp', 'mp'), may hold values from -3 to 3
- key_weight: bfloat16 [4096, 4096], P('dp', 'mp'), may hold values from -1 to 1
- value_weight: bfloat16 [4096, 4096], P('dp', 'mp'), may hold values from -0.09375 to 0.09375
- output_weight: bfloat16 [4096, 4096], P('mp', 'dp'), may hold values from -0.09375 to 0.09375
- cotangent: bfloat16 [2, 256, 4096], P('dp', None, 'mp'), may hold values from -6 to 6
- enc_lengths: int32 [2], P('dp'), may hold values from 64 to 256
- dec_lengths: int32 [2], P('dp'), may hold values from 64 to 256
Outputs:
- layer_out: bfloat16 [2, 256, 4096], P('dp', None, 'mp')
- input_grad: bfloat16 [2, 256, 4096], P('dp', None, 'mp')
- enc_grad: bfloat16 [2, 256, 4096], P('dp', 'mp')
- query_grad: bfloat16 [4096, 4096], P('dp', 'mp')
- key_grad: bfloat16 [4096, 4096], P('dp', 'mp')
- value_grad: bfloat16 [4096, 4096], P('dp', 'mp')
- output_grad: bfloat16 [4096, 4096], P('mp', 'dp')
All inputs are finite; a program needn't handle non-finite values.
Results may differ from a plain program's by a relative error of at most 0.019.
The roundings to bfloat16 on the way count: a program that leaves them out, or rounds other values in their place, can miss the bound.
Values may be sent and summed in bfloat16 or wider, within the bound.
A program may use at most 64 MiB of HBM per device.

v0:
```python
import jax
import jax.numpy as jnp
from jax import lax
from jax.sharding import PartitionSpec as P

DH = 256


def local(
    dec_input,
    enc_output,
    query_weight,
    key_weight,
    value_weight,
    output_weight,
    cotangent,
    enc_lengths,
    dec_lengths,
):
    scale = DH ** (-0.5)
    hidden = lax.all_gather(dec_input, "mp", axis=2, tiled=True)[0]
    query_full, key_full, value_full = (
        lax.all_gather(query_weight, "dp", axis=0, tiled=True),
        lax.all_gather(key_weight, "dp", axis=0, tiled=True),
        lax.all_gather(value_weight, "dp", axis=0, tiled=True),
    )
    output_full = lax.all_gather(output_weight, "dp", axis=1, tiled=True)
    encoded = lax.all_gather(enc_output, "mp", axis=1, tiled=True)[0]
    tokens = hidden.shape[0]
    keys_len = encoded.shape[0]
    width = query_weight.shape[1]
    heads_here = width // DH
    hidden32 = hidden.astype(jnp.float32)
    inv_rms = lax.rsqrt(jnp.mean(hidden32 * hidden32, axis=-1, keepdims=True) + 1e-06)
    normed = (hidden32 * inv_rms).astype(jnp.bfloat16)
    query = jnp.dot(normed, query_full, preferred_element_type=jnp.float32).astype(jnp.bfloat16)
    keyed = jnp.dot(encoded, key_full, preferred_element_type=jnp.float32).astype(jnp.bfloat16)
    valued = jnp.dot(encoded, value_full, preferred_element_type=jnp.float32).astype(jnp.bfloat16)
    query_heads = query.reshape(tokens, heads_here, DH)
    key_heads = keyed.reshape(keys_len, heads_here, DH)
    value_heads = valued.reshape(keys_len, heads_here, DH)
    scores = (
        jnp.einsum("thd,lhd->htl", query_heads, key_heads, preferred_element_type=jnp.float32)
        * scale
    )
    valid = jnp.arange(keys_len, dtype=jnp.int32) < enc_lengths[0]
    scores = jnp.where(valid[None, None, :], scores, -1e30)
    shifted = jnp.exp(scores - jnp.max(scores, axis=-1, keepdims=True))
    probs = shifted / jnp.sum(shifted, axis=-1, keepdims=True)
    probs_low = probs.astype(jnp.bfloat16)
    attended = (
        jnp.einsum("htl,lhd->thd", probs_low, value_heads, preferred_element_type=jnp.float32)
        .reshape(tokens, width)
        .astype(jnp.bfloat16)
    )
    partial_out = jnp.dot(attended, output_full, preferred_element_type=jnp.float32)
    out_share = lax.psum_scatter(
        partial_out.astype(jnp.bfloat16), "mp", scatter_dimension=1, tiled=True
    ).astype(jnp.float32)
    own_input = dec_input[0].astype(jnp.float32)
    layer_out = (own_input + out_share).astype(jnp.bfloat16)[None]
    upstream = lax.all_gather(cotangent, "mp", axis=2, tiled=True)[0]
    keep = (jnp.arange(tokens, dtype=jnp.int32) < dec_lengths[0])[:, None]
    masked = jnp.where(keep, upstream, jnp.zeros_like(upstream))
    own_masked = jnp.where(keep, cotangent[0], jnp.zeros_like(cotangent[0]))
    attended_grad = jnp.dot(masked, output_full.T, preferred_element_type=jnp.float32).astype(
        jnp.bfloat16
    )
    grad_heads = attended_grad.reshape(tokens, heads_here, DH)
    probs_grad = jnp.einsum(
        "thd,lhd->htl", grad_heads, value_heads, preferred_element_type=jnp.float32
    )
    scores_grad = (
        probs * (probs_grad - jnp.sum(probs * probs_grad, axis=-1, keepdims=True)) * scale
    ).astype(jnp.bfloat16)
    q_grad = (
        jnp.einsum("htl,lhd->thd", scores_grad, key_heads, preferred_element_type=jnp.float32)
        .reshape(tokens, width)
        .astype(jnp.bfloat16)
    )
    k_grad = (
        jnp.einsum("htl,thd->lhd", scores_grad, query_heads, preferred_element_type=jnp.float32)
        .reshape(keys_len, width)
        .astype(jnp.bfloat16)
    )
    v_grad = (
        jnp.einsum("htl,thd->lhd", probs_low, grad_heads, preferred_element_type=jnp.float32)
        .reshape(keys_len, width)
        .astype(jnp.bfloat16)
    )
    normed_part = jnp.dot(q_grad, query_full.T, preferred_element_type=jnp.float32)
    feature_width = dec_input.shape[2]
    normed_grad = lax.psum(normed_part.astype(jnp.bfloat16), "mp").astype(jnp.float32)
    stat = jnp.mean(normed_grad * hidden32, axis=-1, keepdims=True)
    full_grad = inv_rms * normed_grad - hidden32 * inv_rms**3 * stat
    start = lax.axis_index("mp") * feature_width
    input_share = lax.dynamic_slice_in_dim(full_grad, start, feature_width, 1)
    input_grad = (own_masked.astype(jnp.float32) + input_share).astype(jnp.bfloat16)[None]
    enc_share = lax.psum_scatter(
        (
            jnp.dot(k_grad, key_full.T, preferred_element_type=jnp.float32)
            + jnp.dot(v_grad, value_full.T, preferred_element_type=jnp.float32)
        ).astype(jnp.bfloat16),
        "mp",
        scatter_dimension=0,
        tiled=True,
    )
    enc_grad = enc_share[None]
    weight_share = lax.psum_scatter(
        jnp.concatenate(
            [
                jnp.dot(normed.T, q_grad, preferred_element_type=jnp.float32),
                jnp.dot(encoded.T, k_grad, preferred_element_type=jnp.float32),
                jnp.dot(encoded.T, v_grad, preferred_element_type=jnp.float32),
                jnp.dot(masked.T, attended, preferred_element_type=jnp.float32),
            ],
            axis=1,
        ).astype(jnp.bfloat16),
        "dp",
        scatter_dimension=0,
        tiled=True,
    ).astype(jnp.float32)
    query_grad = weight_share[:, :width].astype(jnp.bfloat16)
    key_grad = weight_share[:, width : 2 * width].astype(jnp.bfloat16)
    value_grad = weight_share[:, 2 * width : 3 * width].astype(jnp.bfloat16)
    output_grad = weight_share[:, 3 * width :].T.astype(jnp.bfloat16)
    return (layer_out, input_grad, enc_grad, query_grad, key_grad, value_grad, output_grad)


def solution(mesh):
    in_specs = (
        P("dp", None, "mp"),
        P("dp", "mp", None),
        P("dp", "mp"),
        P("dp", "mp"),
        P("dp", "mp"),
        P("mp", "dp"),
        P("dp", None, "mp"),
        P("dp"),
        P("dp"),
    )
    out_specs = (
        P("dp", None, "mp"),
        P("dp", None, "mp"),
        P("dp", "mp", None),
        P("dp", "mp"),
        P("dp", "mp"),
        P("dp", "mp"),
        P("mp", "dp"),
    )
    return jax.shard_map(local, mesh=mesh, in_specs=in_specs, out_specs=out_specs, check_vma=False)
```

profile of v0, /device:TPU:14, one launch (start us, length us, event | category | flops | bytes accessed | tf_op | source)
XLA Modules:
  0.0 617.4 jit_solution(9486938455557465851)
XLA Ops:
  7.2 0.7 all-gather.12.cloned.1.call-update
  7.9 0.7 all-gather.16.cloned.1.call-update
  8.7 0.7 all-gather.8.cloned.1.call-update
  9.4 0.5 all-gather.14.cloned.1.call-update
  10.0 0.5 all-gather.10.cloned.1.call-update
  10.6 0.5 all-gather.18.cloned.1.call-update
  11.2 0.7 all-gather.20.cloned.1.call-update
  13.2 38.8 %all-gather.12.cloned.1.call-done = bf16[1,256,4096]{2,1,0:T(8,128)(2,1)} async-done(((bf16[1,256,256]{2,1,0:T(8,128)(2,1)}), bf16[1,256,4096]{2,1,0:T(8,128)(2,1)}) %all-gather.12.cloned.1.call-update) | async-done | bytes 2097168 | tf_op jit(solution)/shard_map/all_gather | solution.py:21
  52.1 2.1 multiply_reduce_fusion.1
  54.2 31.0 %all-gather.16.cloned.1.call-done = bf16[4096,256]{1,0:T(8,128)(2,1)} async-done(((bf16[2048,256]{1,0:T(8,128)(2,1)}), bf16[4096,256]{1,0:T(8,128)(2,1)}) %all-gather.16.cloned.1.call-update) | async-done | bytes 2097168 | tf_op jit(solution)/shard_map/all_gather | solution.py:24
  85.2 42.7 %all-gather.8.cloned.1.call-done = bf16[1,256,4096]{2,1,0:T(8,128)(2,1)} async-done(((bf16[1,16,4096]{2,1,0:T(8,128)(2,1)}), bf16[1,256,4096]{2,1,0:T(8,128)(2,1)}) %all-gather.8.cloned.1.call-update) | async-done | bytes 2097168 | tf_op jit(solution)/shard_map/all_gather | solution.py:28
  127.8 2.9 fusion.25
  130.8 31.3 %all-gather.14.cloned.1.call-done = bf16[4096,256]{1,0:T(8,128)(2,1)} async-done(((bf16[2048,256]{1,0:T(8,128)(2,1)}), bf16[4096,256]{1,0:T(8,128)(2,1)}) %all-gather.14.cloned.1.call-update) | async-done | bytes 2097168 | tf_op jit(solution)/shard_map/all_gather | solution.py:23
  162.1 2.3 fusion.28
  164.5 0.3 fusion.50
  164.8 31.9 %all-gather.10.cloned.1.call-done = bf16[4096,256]{1,0:T(8,128)(2,1)} async-done(((bf16[2048,256]{1,0:T(8,128)(2,1)}), bf16[4096,256]{1,0:T(8,128)(2,1)}) %all-gather.10.cloned.1.call-update) | async-done | bytes 2097168 | tf_op jit(solution)/shard_map/all_gather | solution.py:25
  196.7 2.9 fusion.22
  199.6 31.6 %all-gather.18.cloned.1.call-done = bf16[256,4096]{1,0:T(8,128)(2,1)} async-done(((bf16[256,2048]{1,0:T(8,128)(2,1)}), bf16[256,4096]{1,0:T(8,128)(2,1)}) %all-gather.18.cloned.1.call-update) | async-done | bytes 2097168 | tf_op jit(solution)/shard_map/all_gather | solution.py:27
  231.2 43.9 %all-gather.20.cloned.1.call-done = bf16[1,256,4096]{2,1,0:T(8,128)(2,1)} async-done(((bf16[1,256,256]{2,1,0:T(8,128)(2,1)}), bf16[1,256,4096]{2,1,0:T(8,128)(2,1)}) %all-gather.20.cloned.1.call-update) | async-done | bytes 2097168 | tf_op jit(solution)/shard_map/all_gather | solution.py:62
  275.1 3.0 fusion.21
  278.1 0.3 multiply_reduce_fusion.2
  278.6 1.0 copy-done.3
  279.7 2.1 convolution_convert_fusion.4
  281.9 0.2 fusion.29
  282.1 3.7 convolution_convert_fusion.5
  286.1 0.2 fusion.32
  286.3 2.6 fusion.1
  288.9 0.7 fusion.2
  289.7 0.9 copy-done.7
  290.5 0.8 convolution_convert_fusion
  291.3 0.8 convolution_convert_fusion.1
  292.1 4.0 pad_maximum_fusion
  296.4 2.5 fusion.51
  299.0 2.1 fusion
  301.1 2.4 convert_bitcast_fusion
  303.5 74.9 %all-reduce.2.cloned.1.call-done = bf16[256,4096]{1,0:T(8,128)(2,1)} async-done(((bf16[256,4096]{1,0:T(8,128)(2,1)}), bf16[256,4096]{1,0:T(8,128)(2,1)}) %all-reduce.2.cloned.1.call-update) | async-done | bytes 2097168 | tf_op jit(solution)/shard_map/psum | solution.py:93
  378.5 2.2 convert_element_type.160
  380.7 0.6 multiply_reduce_fusion
  381.4 0.2 copy-done.6
  381.6 1.8 fusion.43
  383.4 60.7 %reduce-scatter.4.cloned.1.call-done = bf16[256,256]{1,0:T(8,128)(2,1)} async-done(((bf16[256,4096]{1,0:T(8,128)(2,1)}), bf16[256,256]{1,0:T(8,128)(2,1)}) %reduce-scatter.4.cloned.1.call-update) | async-done | bytes 131088 | tf_op jit(solution)/shard_map/reduce_scatter | solution.py:57
  444.1 1.6 fusion.42
  445.7 98.0 %reduce-scatter.8.cloned.1.call-done = bf16[2048,1024]{0,1:T(8,128)(2,1)} async-done(((bf16[4096,1024]{0,1:T(8,128)(2,1)}), bf16[2048,1024]{0,1:T(8,128)(2,1)}) %reduce-scatter.8.cloned.1.call-update) | async-done | bytes 4194320 | tf_op jit(solution)/shard_map/reduce_scatter | solution.py:109
  543.7 3.6 slice_bitcast_fusion
  547.2 1.3 copy.18
  548.5 1.3 copy.17
  549.8 1.3 copy.16
  551.1 59.8 %reduce-scatter.6.cloned.1.call-done = bf16[16,4096]{1,0:T(8,128)(2,1)} async-done(((bf16[256,4096]{1,0:T(8,128)(2,1)}), bf16[16,4096]{1,0:T(8,128)(2,1)}) %reduce-scatter.6.cloned.1.call-update) | async-done | bytes 131088 | tf_op jit(solution)/shard_map/reduce_scatter | solution.py:99
  (36 shorter events, 1.3 us)
Async XLA Ops:
  7.2 44.9 %all-gather.12.cloned.1.call-start = ((), (), s32[]{:S(2)}) async-start(), calls=%async_computation.5 | async-start | bytes 2228224 | tf_op jit(solution)/shard_map/all_gather | solution.py:21
  7.9 77.3 %all-gather.16.cloned.1.call-start = ((), (), s32[]{:S(2)}) async-start(), calls=%async_computation.7 | async-start | bytes 3145728 | tf_op jit(solution)/shard_map/all_gather | solution.py:24
  8.6 119.2 %all-gather.8.cloned.1.call-start = ((), (), s32[]{:S(2)}) async-start(), calls=%async_computation.3 | async-start | bytes 2228224 | tf_op jit(solution)/shard_map/all_gather | solution.py:28
  9.4 152.7 %all-gather.14.cloned.1.call-start = ((), (), s32[]{:S(2)}) async-start(), calls=%async_computation.6 | async-start | bytes 3145728 | tf_op jit(solution)/shard_map/all_gather | solution.py:23
  10.0 186.7 %all-gather.10.cloned.1.call-start = ((), (), s32[]{:S(2)}) async-start(), calls=%async_computation.4 | async-start | bytes 3145728 | tf_op jit(solution)/shard_map/all_gather | solution.py:25
  10.5 220.7 %all-gather.18.cloned.1.call-start = ((), (), s32[]{:S(2)}) async-start(), calls=%async_computation.8 | async-start | bytes 3145728 | tf_op jit(solution)/shard_map/all_gather | solution.py:27
  11.1 264.0 %all-gather.20.cloned.1.call-start = ((), (), s32[]{:S(2)}) async-start(), calls=%async_computation.10 | async-start | bytes 2228224 | tf_op jit(solution)/shard_map/all_gather | solution.py:62
  11.9 366.6 %all-reduce.2.cloned.1.call-start = ((), (), s32[]{:S(2)}) async-start(), calls=%async_computation.11 | async-start | bytes 4194304 | tf_op jit(solution)/shard_map/psum | solution.py:93
  54.1 108.0 %copy-start = (bf16[1,256,4096]{2,1,0:T(8,128)(2,1)S(1)}, bf16[1,256,4096]{2,1,0:T(8,128)(2,1)}, u32[]{:S(2)}) copy-start(bf16[1,256,4096]{2,1,0:T(8,128)(2,1)} %all-gather.12.cloned.1.call-done) | copy-start | bytes 6291460
  278.1 1.6 copy-start.3
  281.8 162.2 %reduce-scatter.4.cloned.1.call-start = ((), (), s32[]{:S(2)}) async-start(), calls=%async_computation.9 | async-start | bytes 2228224 | tf_op jit(solution)/shard_map/reduce_scatter | solution.py:57
  285.8 257.9 %reduce-scatter.8.cloned.1.call-start = ((), (), s32[]{:S(2)}) async-start(), calls=%async_computation.13 | async-start | bytes 12582912 | tf_op jit(solution)/shard_map/reduce_scatter | solution.py:109
  286.3 2.6 copy-start.2
  288.9 1.6 copy-start.7
  296.2 314.7 %reduce-scatter.6.cloned.1.call-start = ((), (), s32[]{:S(2)}) async-start(), calls=%async_computation.12 | async-start | bytes 2228224 | tf_op jit(solution)/shard_map/reduce_scatter | solution.py:99
  296.4 2.6 copy-start.4
  378.4 2.2 copy-start.1
  380.7 0.9 copy-start.6
  380.7 63.4 %copy-start.5 = (bf16[1,256,256]{2,1,0:T(8,128)(2,1)S(1)}, bf16[1,256,256]{2,1,0:T(8,128)(2,1)}, u32[]{:S(2)}) copy-start(bf16[1,256,256]{2,1,0:T(8,128)(2,1)} %param.9) | copy-start | bytes 393220
Sparse Core Ops, SparseCore 0:
  10.2 41.8 all-gather.11
  53.6 31.5 all-gather.15
  87.3 40.4 all-gather.7
  129.2 32.8 all-gather.13
  163.5 33.1 all-gather.9
  198.0 33.1 all-gather.17
  233.4 41.6 all-gather.19
  281.9 96.4 all-reduce.1
  382.7 61.3 reduce-scatter.3
  446.2 97.4 reduce-scatter.7
  548.5 62.3 reduce-scatter.5
where the time goes:
time: 620 us; the launch traced here: 617 us
  waiting for transfers between devices  549 us (89%)
  matrix products  28 us (5%)
  between operations  15.4 us (2%)
  other arithmetic  15 us (2%)
  local copies, waits for them, and re-layouts  9.59 us (2%)
    reduce_scatter x1, waiting for transfers between devices, local(): lax.psum_scatter(jnp.concatenate([jnp.dot(normed.T, q_grad, preferred_ele...  98 us
    psum x1, waiting for transfers between devices, local(): lax.psum(normed_part.astype(jnp.bfloat16), 'mp').astype(jnp.float32)  74.9 us
    reduce_scatter x1, waiting for transfers between devices, local(): lax.psum_scatter(partial_out.astype(jnp.bfloat16), 'mp', scatter_dimensio...  60.7 us
    reduce_scatter x1, waiting for transfers between devices, local(): lax.psum_scatter((jnp.dot(k_grad, key_full.T, preferred_element_type=jnp....  59.8 us
    all_gather x1, waiting for transfers between devices, local(): upstream = lax.all_gather(cotangent, 'mp', axis=2, tiled=True)[0]  43.9 us
    all_gather x1, waiting for transfers between devices, local(): encoded = lax.all_gather(enc_output, 'mp', axis=1, tiled=True)[0]  42.7 us
    all_gather x1, waiting for transfers between devices, local(): hidden = lax.all_gather(dec_input, 'mp', axis=2, tiled=True)[0]  38.8 us
    all_gather x1, waiting for transfers between devices, local(): lax.all_gather(value_weight, 'dp', axis=0, tiled=True)  31.9 us
  transfers between devices with their start and end apart: 11, of which 11 were waited for; matrix products, arithmetic and copies ran while one was open for 7% of the time, Pallas kernels for 0%

commit v1 on v0

--- a/solution.py
+++ b/solution.py
@@ -1,9 +1,16 @@
+import functools
+
 import jax
 import jax.numpy as jnp
 from jax import lax
+from jax.experimental import pallas as pl
+from jax.experimental.pallas import tpu as pltpu
 from jax.sharding import PartitionSpec as P
 
 DH = 256
+MESH = pl.DeviceIdType.MESH
+F32 = jnp.float32
+BF16 = jnp.bfloat16
 
 
 def local(
@@ -127,6 +134,444 @@
     return (layer_out, input_grad, enc_grad, query_grad, key_grad, value_grad, output_grad)
 
 
+NZ = 4
+
+
+def place():
+    y, m = lax.axis_index("dp"), lax.axis_index("mp")
+    z, x, c = m // 4, (m // 2) % 2, m % 2
+    peers = {
+        "up": (y, m + 4),
+        "down": (y, m - 4),
+        "y": (1 - y, m),
+        "x": (y, m + 2 - 4 * x),
+        "c": (y, m + 1 - 2 * c),
+    }
+    return y, z, x, c, peers
+
+
+def greet(z, peers):
+    barrier = pltpu.get_barrier_semaphore()
+    for way in ("y", "x", "c"):
+        pl.semaphore_signal(barrier, inc=1, device_id=peers[way], device_id_type=MESH)
+
+    @pl.when(z < NZ - 1)
+    def _():
+        pl.semaphore_signal(barrier, inc=1, device_id=peers["up"], device_id_type=MESH)
+
+    @pl.when(z > 0)
+    def _():
+        pl.semaphore_signal(barrier, inc=1, device_id=peers["down"], device_id_type=MESH)
+
+    inner = ((z + 1) // 2) % 2
+    pl.semaphore_wait(barrier, 4 + inner)
+
+
+def when(pred, act):
+    if pred is None:
+        act()
+    else:
+        pl.when(pred)(act)
+
+
+def both(a, b):
+    return b if a is None else a if b is None else jnp.logical_and(a, b)
+
+
+class Sends:
+    def __init__(self):
+        self.open = []
+
+    def start(self, pred, src, dst, sems, at, peer):
+        copy = pltpu.make_async_remote_copy(
+            src_ref=src,
+            dst_ref=dst,
+            send_sem=sems.at[0, at],
+            recv_sem=sems.at[1, at],
+            device_id=peer,
+            device_id_type=MESH,
+        )
+        when(pred, lambda: copy.start())
+        self.open.append((pred, copy))
+
+    def finish(self):
+        for pred, copy in self.open:
+            when(pred, lambda copy=copy: copy.wait_send())
+
+
+def arrived(pred, dst, sems, at, peer):
+    copy = pltpu.make_async_remote_copy(
+        src_ref=dst,
+        dst_ref=dst,
+        send_sem=sems.at[0, at],
+        recv_sem=sems.at[1, at],
+        device_id=peer,
+        device_id_type=MESH,
+    )
+    when(pred, lambda: copy.wait_recv())
+
+
+def feature_block(ref, s, j, x, c):
+    return ref.at[s, :, pl.ds(pl.multiple_of(j * 1024 + x * 512 + c * 256, 256), 256)]
+
+
+def row_block(ref, s, j, x, c):
+    return ref.at[s, pl.ds(pl.multiple_of(j * 64 + x * 32 + c * 16, 16), 16), :]
+
+
+def gather_kernel(dec, enc, cot, gd, ge, gc, *sems):
+    y, z, x, c, peers = place()
+    sends = Sends()
+    local_sems, sems = sems[0], sems[1:]
+    tensors = []
+    for t, (own, out, rows) in enumerate(((dec, gd, False), (enc, ge, True), (cot, gc, False))):
+        up, down, ys, xs, cs = sems[5 * t : 5 * t + 5]
+        tensors.append((t, own, out, rows, up, down, ys, xs, cs))
+
+    def held(tensor, zz):
+        _, own, out, rows = tensor[:4]
+        if rows:
+            return [
+                (row_block(out, y, zz, x, c), True),
+                (row_block(out, 2, zz, x, c), False),
+            ]
+        other = (zz // 2 + y) % 2
+        slot = y + (2 - y) * other
+        return [(feature_block(out, slot, zz % 2, x, c), other)]
+
+    def onward(tensor, zz, pred, own=None):
+        t, _, out, rows, up, down, ys, xs, cs = tensor
+        if rows:
+            mine = row_block(out, y, zz, x, c)
+            far = row_block(out, 2, zz, x, c)
+            src, src_far = (mine, far) if own is None else own
+            sends.start(pred, src_far, mine, ys, zz, peers["y"])
+            sends.start(pred, src, mine, xs, y * 4 + zz, peers["x"])
+            sends.start(pred, src, mine, cs, (y * 4 + zz) * 2 + x, peers["c"])
+            return
+        other = (zz // 2 + y) % 2
+        j = zz % 2
+        slot = y + (2 - y) * other
+        src = feature_block(out, slot, j, x, c) if own is None else own
+        mine = feature_block(out, y, j, x, c)
+        sends.start(both(pred, other == 1), src, mine, ys, j, peers["y"])
+        near = both(pred, other == 0)
+        sends.start(near, src, mine, xs, y * 2 + j, peers["x"])
+        sends.start(near, src, mine, cs, (y * 2 + j) * 2 + x, peers["c"])
+
+    greet(z, peers)
+    local = []
+    for tensor in tensors:
+        t, own, out, rows, up, down = tensor[:6]
+        views = [view for view, _ in held(tensor, z)]
+        if rows:
+            half = lambda h: own.at[:, pl.ds(pl.multiple_of(h * 2048, 2048), 2048)]
+            srcs = [half(y), half(1 - y)]
+        else:
+            srcs = [own]
+        n = len(views)
+        for i, (src, view) in enumerate(zip(srcs, views)):
+            sends.start(z < NZ - 1, src, view, up, i, peers["up"])
+            sends.start(z > 0, src, view, down, i, peers["down"])
+        onward(tensor, z, None, tuple(srcs) if rows else srcs[0])
+        for i, (src, view) in enumerate(zip(srcs, views)):
+            copy = pltpu.make_async_copy(src, view, local_sems.at[2 * t + i])
+            copy.start()
+            local.append(copy)
+    for k in range(NZ - 1):
+        for tensor in tensors:
+            t, own, out, rows, up, down = tensor[:6]
+            below, above = z - 1 - k, z + 1 + k
+            has_below, has_above = below >= 0, above < NZ
+            low = jnp.maximum(below, 0)
+            high = jnp.minimum(above, NZ - 1)
+            for zz, ok, sems_way, way, more in (
+                (low, has_below, up, "up", z < NZ - 1),
+                (high, has_above, down, "down", z > 0),
+            ):
+                views = [view for view, _ in held(tensor, zz)]
+                n = len(views)
+                for i, view in enumerate(views):
+                    arrived(ok, view, sems_way, k * n + i, peers["c"])
+                    if k + 1 < NZ - 1:
+                        sends.start(both(ok, more), view, view, sems_way, (k + 1) * n + i, peers[way])
+                onward(tensor, zz, ok)
+    for tensor in tensors:
+        t, own, out, rows, up, down, ys, xs, cs = tensor
+        block = row_block if rows else feature_block
+        n = 4 if rows else 2
+        for j in range(n):
+            view = block(out, 1 - y, j, x, c)
+            arrived(None, view, ys, j, peers["y"])
+            sends.start(None, view, view, xs, (1 - y) * n + j, peers["x"])
+            sends.start(None, view, view, cs, ((1 - y) * n + j) * 2 + x, peers["c"])
+    for tensor in tensors:
+        t, own, out, rows, up, down, ys, xs, cs = tensor
+        block = row_block if rows else feature_block
+        n = 4 if rows else 2
+        for j in range(n):
+            for s in (y, 1 - y):
+                view = block(out, s, j, 1 - x, c)
+                arrived(None, view, xs, s * n + j, peers["x"])
+                sends.start(None, view, view, cs, (s * n + j) * 2 + 1 - x, peers["c"])
+    for tensor in tensors:
+        t, own, out, rows, up, down, ys, xs, cs = tensor
+        block = row_block if rows else feature_block
+        n = 4 if rows else 2
+        for s in range(2):
+            for j in range(n):
+                for xx in range(2):
+                    arrived(None, block(out, s, j, xx, 1 - c), cs, (s * n + j) * 2 + xx, peers["c"])
+    for copy in local:
+        copy.wait()
+    sends.finish()
+
+
+def gather(dec, enc, cot):
+    vmem = pl.BlockSpec(memory_space=pltpu.VMEM)
+    out = jax.ShapeDtypeStruct((3, 256, 2048), BF16)
+    sems = [pltpu.SemaphoreType.DMA((6,))]
+    for rows in (False, True, False):
+        n = 2 if rows else 1
+        counts = (3 * n, 3 * n, 2 * n, 4 * n, 8 * n)
+        sems += [pltpu.SemaphoreType.DMA((2, count)) for count in counts]
+    return pl.pallas_call(
+        gather_kernel,
+        out_shape=(out, out, out),
+        in_specs=[vmem] * 3,
+        out_specs=(vmem,) * 3,
+        scratch_shapes=sems,
+        compiler_params=pltpu.CompilerParams(
+            collective_id=0, has_side_effects=True, vmem_limit_bytes=40 * 2**20
+        ),
+        name="gather_activations",
+    )(dec, enc, cot)
+
+
+def scatter_kernel(po, ng, eg, out_o, out_n, out_e, *scratch):
+    y, z, x, c, peers = place()
+    sends = Sends()
+    tensors = []
+    for t, (part, out, rows) in enumerate(((po, out_o, False), (ng, out_n, False), (eg, out_e, True))):
+        tensors.append((part, out, rows) + tuple(scratch[15 * t : 15 * t + 15]))
+
+    greet(z, peers)
+    for part, out, rows, rc, ax, rx, by, ry, v, su, ru, sd, rd, cs, xs, ys, us, ds in tensors:
+        block = row_block if rows else feature_block
+        n = 4 if rows else 2
+        for xx in (1 - x, x):
+            for s in (1 - y, y):
+                for j in range(n):
+                    at = (s * n + j) * 2 + xx
+                    sends.start(None, block(part, s, j, xx, 1 - c), rc.at[at], cs, at, peers["c"])
+
+    def across_x(tensor):
+        part, out, rows, rc, ax, rx, by, ry, v, su, ru, sd, rd, cs, xs, ys, us, ds = tensor
+        block = row_block if rows else feature_block
+        n = 4 if rows else 2
+        for s in (1 - y, y):
+            for j in range(n):
+                at = (s * n + j) * 2 + 1 - x
+                arrived(None, rc.at[at], cs, at, peers["c"])
+                own = block(part, s, j, 1 - x, c)[...].astype(F32)
+                ax[s * n + j] = (own + rc[at].astype(F32)).astype(BF16)
+                sends.start(None, ax.at[s * n + j], rx.at[s * n + j], xs, s * n + j, peers["x"])
+
+    def across_y(tensor):
+        part, out, rows, rc, ax, rx, by, ry, v, su, ru, sd, rd, cs, xs, ys, us, ds = tensor
+        block = row_block if rows else feature_block
+        n = 4 if rows else 2
+        for s in (1 - y, y):
+            for j in range(n):
+                at = (s * n + j) * 2 + x
+                arrived(None, rc.at[at], cs, at, peers["c"])
+                arrived(None, rx.at[s * n + j], xs, s * n + j, peers["x"])
+                own = block(part, s, j, x, c)[...].astype(F32)
+                total = own + rc[at].astype(F32) + rx[s * n + j].astype(F32)
+                if s is not y:
+                    by[j] = total.astype(BF16)
+                    sends.start(None, by.at[j], ry.at[j], ys, j, peers["y"])
+                elif rows:
+                    v[j, :, pl.ds(pl.multiple_of(y * 2048, 2048), 2048)] = total
+                else:
+                    v[2 * y + j] = total
+
+    def along_z(tensor):
+        part, out, rows, rc, ax, rx, by, ry, v, su, ru, sd, rd, cs, xs, ys, us, ds = tensor
+        n = 4 if rows else 2
+        for j in range(n):
+            arrived(None, ry.at[j], ys, j, peers["y"])
+            if rows:
+                v[j, :, pl.ds(pl.multiple_of((1 - y) * 2048, 2048), 2048)] = ry[j].astype(F32)
+            else:
+                v[2 * (1 - y) + j] = ry[j].astype(F32)
+        for k in range(NZ):
+            for at, buf, sbuf, sems, way, got, on in (
+                (NZ - 1 - k, ru, su, us, "up", (z > 0) & (z <= NZ - 1 - k), z < NZ - 1 - k),
+                (k, rd, sd, ds, "down", (z < NZ - 1) & (z >= k), z > k),
+            ):
+                if not (way == "up" and at == 0) and not (way == "down" and at == NZ - 1):
+                    arrived(got, buf.at[at], sems, at, peers["c"])
+                    more = got & on
+
+                    @pl.when(more)
+                    def _(at=at, buf=buf, sbuf=sbuf):
+                        sbuf[at] = (v[at] + buf[at].astype(F32)).astype(BF16)
+
+                    @pl.when(jnp.logical_and(on, jnp.logical_not(got)))
+                    def _(at=at, sbuf=sbuf):
+                        sbuf[at] = v[at].astype(BF16)
+
+                    sends.start(on, sbuf.at[at], buf.at[at], sems, at, peers[way])
+        out[...] = v[z]
+
+        @pl.when(z > 0)
+        def _():
+            out[...] += ru[z].astype(F32)
+
+        @pl.when(z < NZ - 1)
+        def _():
+            out[...] += rd[z].astype(F32)
+
+    for tensor in tensors:
+        across_x(tensor)
+    for i, tensor in enumerate(tensors):
+        across_y(tensor)
+        if i:
+            along_z(tensors[i - 1])
+    along_z(tensors[-1])
+    sends.finish()
+
+
+def scatter(po, ng, eg):
+    vmem = pl.BlockSpec(memory_space=pltpu.VMEM)
+    scratch = []
+    for rows in (False, False, True):
+        n = 4 if rows else 2
+        r, w, wz = (16, 2048, 4096) if rows else (256, 256, 256)
+        scratch += [
+            pltpu.VMEM((4 * n, r, w), BF16),
+            pltpu.VMEM((2 * n, r, w), BF16),
+            pltpu.VMEM((2 * n, r, w), BF16),
+            pltpu.VMEM((n, r, w), BF16),
+            pltpu.VMEM((n, r, w), BF16),
+            pltpu.VMEM((NZ, r, wz), F32),
+        ]
+        scratch += [pltpu.VMEM((NZ, r, wz), BF16)] * 4
+        scratch += [pltpu.SemaphoreType.DMA((2, k)) for k in (4 * n, 2 * n, n, NZ, NZ)]
+    return pl.pallas_call(
+        scatter_kernel,
+        out_shape=(
+            jax.ShapeDtypeStruct((256, 256), F32),
+            jax.ShapeDtypeStruct((256, 256), F32),
+            jax.ShapeDtypeStruct((16, 4096), F32),
+        ),
+        in_specs=[vmem] * 3,
+        out_specs=(vmem,) * 3,
+        scratch_shapes=scratch,
+        compiler_params=pltpu.CompilerParams(
+            collective_id=1, has_side_effects=True, vmem_limit_bytes=48 * 2**20
+        ),
+        name="reduce_scatter",
+    )(po, ng, eg)
+
+
+def dot(a, b, dims):
+    return lax.dot_general(a, b, (dims, ((), ())), preferred_element_type=F32)
+
+
+def swap(a):
+    return lax.ppermute(a, "dp", [(0, 1), (1, 0)])
+
+
+def fast(
+    dec_input,
+    enc_output,
+    query_weight,
+    key_weight,
+    value_weight,
+    output_weight,
+    cotangent,
+    enc_lengths,
+    dec_lengths,
+):
+    y = lax.axis_index("dp")
+    scale = DH ** (-0.5)
+    tokens = dec_input.shape[1]
+    width = NZ * 4 * dec_input.shape[2]
+    half = query_weight.shape[0]
+    keep = (jnp.arange(tokens, dtype=jnp.int32) < dec_lengths[0])[:, None]
+    own_masked = jnp.where(keep, cotangent[0], jnp.zeros_like(cotangent[0]))
+    hidden, encoded, masked = gather(dec_input[0], enc_output[0], own_masked)
+    hidden, encoded, masked = (
+        hidden[:2].astype(F32),
+        encoded[:2].reshape(-1, half),
+        masked[:2].reshape(-1, half),
+    )
+    squares = jnp.sum(hidden * hidden, axis=-1)
+    inv_rms = lax.rsqrt((squares + swap(squares)) / width + 1e-06)
+    normed = (hidden * inv_rms[:, :, None]).astype(BF16).reshape(-1, half)
+
+    def own(parts):
+        return lax.dynamic_index_in_dim(parts, y, 0, keepdims=False)
+
+    def project(left, weight, dims):
+        parts = dot(left, weight, dims).reshape(2, -1, weight.shape[1 - dims[1][0]])
+        theirs = lax.dynamic_index_in_dim(parts, 1 - y, 0, keepdims=False)
+        return (own(parts) + swap(theirs)).astype(BF16)
+
+    down = ((1,), (0,))
+    keyed = project(encoded, key_weight, down)
+    valued = project(encoded, value_weight, down)
+    query = project(normed, query_weight, down)
+    attended_grad = project(masked, output_weight, ((1,), (1,)))
+
+    scores = dot(query, keyed, ((1,), (1,))) * scale
+    valid = jnp.arange(keyed.shape[0], dtype=jnp.int32) < enc_lengths[0]
+    scores = jnp.where(valid[None, :], scores, -1e30)
+    shifted = jnp.exp(scores - jnp.max(scores, axis=-1, keepdims=True))
+    probs = shifted / jnp.sum(shifted, axis=-1, keepdims=True)
+    probs_low = probs.astype(BF16)
+    attended = dot(probs_low, valued, down).astype(BF16)
+    probs_grad = dot(attended_grad, valued, ((1,), (1,)))
+    scores_grad = (
+        probs * (probs_grad - jnp.sum(probs * probs_grad, axis=-1, keepdims=True)) * scale
+    ).astype(BF16)
+    q_grad = dot(scores_grad, keyed, down).astype(BF16)
+    k_grad = dot(scores_grad, query, ((0,), (0,))).astype(BF16)
+    v_grad = dot(probs_low, attended_grad, ((0,), (0,))).astype(BF16)
+
+    def pair(mine):
+        theirs = swap(mine)
+        first = jnp.where(y == 0, mine, theirs)
+        second = jnp.where(y == 0, theirs, mine)
+        return jnp.concatenate([first, second], axis=0)
+
+    v_both, att_both, q_both, k_both = pair(v_grad), pair(attended), pair(q_grad), pair(k_grad)
+    part_out = dot(att_both, output_weight, down).astype(BF16).reshape(2, -1, half)
+    part_normed = dot(q_both, query_weight, ((1,), (1,))).astype(BF16).reshape(2, -1, half)
+    part_enc = (
+        dot(k_both, key_weight, ((1,), (1,))) + dot(v_both, value_weight, ((1,), (1,)))
+    ).astype(BF16).reshape(2, -1, half)
+    stats = lax.psum(jnp.sum(part_normed.astype(F32) * hidden, axis=-1), ("dp", "mp")) / width
+    out_sum, normed_grad, enc_sum = scatter(part_out, part_normed, part_enc)
+
+    rows = ((0,), (0,))
+    query_grad = dot(normed, q_both, rows).astype(BF16)
+    key_grad = dot(encoded, k_both, rows).astype(BF16)
+    value_grad = dot(encoded, v_both, rows).astype(BF16)
+    output_grad = dot(att_both, masked, rows).astype(BF16)
+
+    own_input = dec_input[0].astype(F32)
+    layer_out = (own_input + out_sum).astype(BF16)[None]
+    inv, stat = own(inv_rms)[:, None], own(stats)[:, None]
+    input_grad = (
+        own_masked.astype(F32) + inv * normed_grad - own_input * inv**3 * stat
+    ).astype(BF16)[None]
+    enc_grad = enc_sum.astype(BF16)[None]
+    return (layer_out, input_grad, enc_grad, query_grad, key_grad, value_grad, output_grad)
+
+
 def solution(mesh):
     in_specs = (
         P("dp", None, "mp"),
@@ -148,4 +593,5 @@
         P("dp", "mp"),
         P("mp", "dp"),
     )
-    return jax.shard_map(local, mesh=mesh, in_specs=in_specs, out_specs=out_specs, check_vma=False)
+    program = fast if dict(mesh.shape) == {"dp": 2, "mp": 16} else local
+    return jax.shard_map(program, mesh=mesh, in_specs=in_specs, out_specs=out_specs, check_vma=False)

time: 620 us -> 303 us (0.49)
  waiting for transfers between devices: 549 us -> 7.41 us
  Pallas kernels: 0 us -> 181 us
  blocking collectives: 0 us -> 48.7 us
  between operations: 15.4 us -> 2.5 us
  local copies, waits for them, and re-layouts: 9.59 us -> 17.8 us
  starting transfers between devices: 0.61 us -> 8.3 us
    all_gather x7 -> x0, waiting for transfers between devices: 251 us -> none  [the longest x1 43.9 us: local(): upstream = lax.all_gather(cotangent, 'mp', axis=2, tiled=True)[0]]
    reduce_scatter x3 -> x0, waiting for transfers between devices: 218 us -> none  [the longest x1 98 us: local(): lax.psum_scatter(jnp.concatenate([jnp.dot(normed.T, q_grad, preferred_ele...]
    pallas_call x0 -> x2, Pallas kernels: none -> 179 us  [the longest x1 135 us: scatter(): pl.pallas_call(scatter_kernel, out_shape=(jax.ShapeDtypeStruct((256, 256)...]
    psum x1 -> x0, waiting for transfers between devices: 74.9 us -> none  [local(): lax.psum(normed_part.astype(jnp.bfloat16), 'mp').astype(jnp.float32)]
    psum x0 -> x1, blocking collectives: none -> 48.7 us  [fast(): lax.psum(jnp.sum(part_normed.astype(F32) * hidden, axis=-1), ('dp', 'mp'))]
    ppermute x0 -> x9, starting transfers between devices: none -> 8.3 us  [swap(): return lax.ppermute(a, 'dp', [(0, 1), (1, 0)])]
    ppermute x0 -> x9, waiting for transfers between devices: none -> 7.41 us  [swap(): return lax.ppermute(a, 'dp', [(0, 1), (1, 0)])]
    unnamed x19 -> x70, local copies, waits for them, and re-layouts: 6.03 us -> 12.9 us
  transfers between devices with their start and end apart: 11 -> 9, of which waited for: 11 -> 3; matrix products, arithmetic and copies ran while one was open for 7% -> 9% of each run, Pallas kernels for 0% -> 0%
where the time goes in v1:
time: 303 us; the launch traced here: 302 us
  Pallas kernels  181 us (60%)
  blocking collectives  48.7 us (16%)
  matrix products  24.6 us (8%)
  local copies, waits for them, and re-layouts  17.8 us (6%)
  other arithmetic  11.6 us (4%)
  starting transfers between devices  8.3 us (3%)
  waiting for transfers between devices  7.41 us (2%)
    pallas_call x1, Pallas kernels, scatter(): pl.pallas_call(scatter_kernel, out_shape=(jax.ShapeDtypeStruct((256, 256)...  135 us
    psum x1, blocking collectives, fast(): lax.psum(jnp.sum(part_normed.astype(F32) * hidden, axis=-1), ('dp', 'mp'))  48.7 us
    pallas_call x1, Pallas kernels, gather(): pl.pallas_call(gather_kernel, out_shape=(out, out, out), in_specs=[vmem]...  43.6 us
    dot_general x17, matrix products, dot(): return lax.dot_general(a, b, (dims, ((), ())), preferred_element_type=F32)  24.6 us
    unnamed x70, local copies, waits for them, and re-layouts  12.9 us
    ppermute x9, starting transfers between devices, swap(): return lax.ppermute(a, 'dp', [(0, 1), (1, 0)])  8.3 us
    ppermute x9, waiting for transfers between devices, swap(): return lax.ppermute(a, 'dp', [(0, 1), (1, 0)])  7.41 us
  transfers between devices with their start and end apart: 9, of which 3 were waited for; matrix products, arithmetic and copies ran while one was open for 9% of the time, Pallas kernels for 0%

profile of v1, /device:TPU:14, one launch (start us, length us, event | category | flops | bytes accessed | tf_op | source)
XLA Modules:
  0.0 301.8 jit_solution(8120392388602678840)
XLA Ops:
  1.4 1.0 bitcast_select_fusion.cot
  2.4 0.9 copy-done.8
  3.3 0.9 copy-done.10
  4.2 43.6 %gather_activations.1 = (bf16[3,256,2048]{2,1,0:T(8,128)(2,1)S(1)}, bf16[3,256,2048]{2,1,0:T(8,128)(2,1)S(1)}, bf16[3,256,2048]{2,1,0:T(8,128)(2,1)S(1)}) custom-call(bf16[256,256]{1,0:T(8,128)(2,1)S(1)} %bitcast.83, bf16[16,4096]{1,0:T(8,128)(2,1)S(1)} %bitcast.84, bf16[256,256]{1,0:T(8,128)(2,1)S(1)} %bitcast_select_fusion.cot), custom_call_target="tpu_custom_call" | custom-call | tf_op jit(solution)/shard_map/gather_activations/pallas_call | solution.py:338
  47.9 1.7 copy-done.4
  49.5 1.7 copy-done.7
  51.3 1.6 copy-done.1
  53.5 2.5 fusion.4
  56.0 0.8 dynamic-slice_bitcast_fusion
  56.8 2.0 collective-permute-start.5
  58.8 0.7 fusion.6
  59.5 0.7 copy-done.30
  60.3 0.7 fusion.8
  61.1 0.8 copy-done.28
  61.9 0.7 dynamic-slice_bitcast_fusion.2
  62.6 2.0 collective-permute-start.2
  65.2 1.9 slice.11
  67.7 1.5 slice.10
  69.3 2.1 fusion.1
  71.4 0.7 fusion.10
  72.8 1.6 fusion.16
  74.5 3.0 collective-permute-done.2
  77.4 1.0 fusion.17
  78.4 1.7 bitcast_add_fusion.1
  80.1 2.5 collective-permute-done.1
  82.7 0.6 copy-done.18
  84.4 2.1 online-softmax
  86.5 1.5 multiply_reduce_fusion
  87.9 1.1 multiply_convert_fusion
  89.1 1.1 convolution_convert_fusion.7
  90.4 1.8 collective-permute-start.4
  92.5 1.7 collective-permute-start.7
  95.0 1.9 collective-permute-done.4
  96.9 2.1 convolution_convert_fusion.1
  99.0 1.7 convolution_convert_fusion.2
  100.8 0.7 convolution_convert_fusion
  101.5 1.1 copy-done.2
  102.6 0.7 fusion.2
  103.3 0.9 copy-done.17
  104.2 1.7 convolution_convert_fusion.5
  106.0 2.7 fusion.21
  108.7 1.9 convolution_convert_fusion.3
  110.7 48.7 %psum.7 = f32[2,256]{1,0:T(2,128)S(1)} all-reduce(f32[2,256]{1,0:T(2,128)S(1)} %fusion.2), channel_id=1, replica_groups=mesh['dp'=2,'mp'=16] {'dp','mp'}, use_global_device_ids=true, to_apply=%region_5.6 | all-reduce | flops 512 | bytes 4096 | tf_op jit(solution)/shard_map/psum | solution.py:556
  159.4 3.5 %convolution_convert_fusion.4 = bf16[2048,256]{1,0:T(8,128)(2,1)} fusion(bf16[512,2048]{1,0:T(8,128)(2,1)} %bitcast.87, bf16[256,256]{1,0:T(8,128)(2,1)S(1)} %get-tuple-element.20, bf16[256,256]{1,0:T(8,128)(2,1)S(1)} %get-tuple-element.19), kind=kOutput, calls=%fused_computation.11 | convolution fusion | flops 537919488 | bytes 3407872 | tf_op jit(solution)/shard_map/dot_general | solution.py:480
  162.9 2.1 add_convert_fusion
  165.0 135.3 %reduce_scatter.1 = (f32[256,256]{1,0:T(8,128)S(1)}, f32[256,256]{1,0:T(8,128)S(1)}, f32[16,4096]{1,0:T(8,128)S(1)}) custom-call(bf16[2,256,2048]{2,1,0:T(8,128)(2,1)S(1)} %bitcast.82, bf16[2,256,2048]{2,1,0:T(8,128)(2,1)S(1)} %bitcast.81, bf16[2,256,2048]{2,1,0:T(8,128)(2,1)} %bitcast.86), custom_call_target="tpu_custom_call" | custom-call | tf_op jit(solution)/shard_map/reduce_scatter/pallas_call | solution.py:462
  300.3 0.7 convert_bitcast_fusion
  300.9 0.9 fusion.22
  (90 shorter events, 4.5 us)
Async XLA Ops:
  0.6 52.8 %copy-start = (bf16[256,2048]{1,0:T(8,128)(2,1)S(1)}, bf16[256,2048]{1,0:T(8,128)(2,1)}, u32[]{:S(2)}) copy-start(bf16[256,2048]{1,0:T(8,128)(2,1)} %param.14) | copy-start | bytes 3145732
  1.4 1.0 copy-start.33
  2.4 0.9 copy-start.8
  3.3 0.9 copy-start.10
  47.8 1.7 copy-start.4
  49.5 1.7 copy-start.7
  51.2 1.6 copy-start.1
  53.4 15.9 %collective-permute-start = (f32[2,256]{1,0:T(2,128)S(1)}, f32[2,256]{1,0:T(2,128)S(1)}, u32[]{:S(2)}, u32[]{:S(2)}) collective-permute-start(f32[2,256]{1,0:T(2,128)S(1)} %fusion), channel_id=1, source_target_pairs={{0,16},{16,0},{1,17},{17,1},{2,18},{18,2},{3,19},{19,3},{4,20},{20... | collective-permute-start | bytes 6152 | tf_op jit(solution)/shard_map/ppermute | solution.py:484
  53.5 5.3 %copy-start.5 = (bf16[3,256,2048]{2,1,0:T(8,128)(2,1)S(1)}, bf16[3,256,2048]{2,1,0:T(8,128)(2,1)}, u32[]{:S(2)}) copy-start(bf16[3,256,2048]{2,1,0:T(8,128)(2,1)} %copy-done.4) | copy-start | bytes 9437188
  53.5 5.3 %copy-start.21 = (bf16[2048,256]{1,0:T(8,128)(2,1)S(1)}, bf16[2048,256]{1,0:T(8,128)(2,1)}, u32[]{:S(2)}) copy-start(bf16[2048,256]{1,0:T(8,128)(2,1)} %param.13) | copy-start | bytes 3145732
  56.0 3.5 %copy-start.26 = (f32[2,256,256]{2,1,0:T(8,128)}, f32[2,256,256]{2,1,0:T(8,128)S(1)}, u32[]{:S(2)}) copy-start(f32[2,256,256]{2,1,0:T(8,128)S(1)} %fusion.4) | copy-start | bytes 1572868
  56.8 16.0 %collective-permute-start.5 = (f32[256,256]{1,0:T(8,128)}, f32[256,256]{1,0:T(8,128)}, u32[]{:S(2)}, u32[]{:S(2)}) collective-permute-start(f32[256,256]{1,0:T(8,128)} %dynamic-slice_bitcast_fusion), channel_id=1, source_target_pairs={{0,16},{16,0},{1,17},{17,1},{2,18},{18,2},{3,19},{19,3},{4,20},{20... | collective-permute-start | bytes 786440 | tf_op jit(solution)/shard_map/ppermute | solution.py:484
  58.8 1.6 copy-start.23
  59.5 0.8 copy-start.30
  60.3 18.1 %collective-permute-start.3 = (f32[256,256]{1,0:T(8,128)S(1)}, f32[256,256]{1,0:T(8,128)}, u32[]{:S(2)}, u32[]{:S(2)}) collective-permute-start(f32[256,256]{1,0:T(8,128)S(1)} %dynamic-slice_bitcast_fusion.1), channel_id=1, source_target_pairs={{0,16},{16,0},{1,17},{17,1},{2,18},{18,2},{3,19},{19,3},{4,20},{20... | collective-permute-start | bytes 786440 | tf_op jit(solution)/shard_map/ppermute | solution.py:484
  61.1 0.8 copy-start.28
  62.6 14.8 %collective-permute-start.2 = (f32[256,256]{1,0:T(8,128)}, f32[256,256]{1,0:T(8,128)}, u32[]{:S(2)}, u32[]{:S(2)}) collective-permute-start(f32[256,256]{1,0:T(8,128)} %dynamic-slice_bitcast_fusion.2), channel_id=1, source_target_pairs={{0,16},{16,0},{1,17},{17,1},{2,18},{18,2},{3,19},{19,3},{4,20},{20... | collective-permute-start | bytes 786440 | tf_op jit(solution)/shard_map/ppermute | solution.py:484
  65.2 2.5 copy-start.6
  69.3 2.1 copy-start.19
  71.4 1.4 copy-start.16
  71.4 1.4 copy-start.27
  71.4 6.0 %copy-start.29 = (f32[2,256,256]{2,1,0:T(8,128)S(1)}, f32[2,256,256]{2,1,0:T(8,128)}, u32[]{:S(2)}) copy-start(f32[2,256,256]{2,1,0:T(8,128)} %copy-done.28) | copy-start | bytes 1572868
  71.4 7.0 %copy-start.31 = (f32[2,256,256]{2,1,0:T(8,128)S(1)}, f32[2,256,256]{2,1,0:T(8,128)}, u32[]{:S(2)}) copy-start(f32[2,256,256]{2,1,0:T(8,128)} %copy-done.30) | copy-start | bytes 1572868
  72.7 9.9 %collective-permute-start.1 = (f32[256,256]{1,0:T(8,128)S(1)}, f32[256,256]{1,0:T(8,128)S(1)}, u32[]{:S(2)}, u32[]{:S(2)}) collective-permute-start(f32[256,256]{1,0:T(8,128)S(1)} %dynamic-slice_bitcast_fusion.3), channel_id=1, source_target_pairs={{0,16},{16,0},{1,17},{17,1},{2,18},{18,2},{3,19},{19,3},{4,20},{20... | collective-permute-start | bytes 786440 | tf_op jit(solution)/shard_map/ppermute | solution.py:484
  82.7 0.7 copy-start.18
  83.6 0.7 copy-start.12
  86.5 3.9 %copy-start.14 = (f32[256,256]{1,0:T(8,128)S(1)}, f32[256,256]{1,0:T(8,128)}, u32[]{:S(2)}) copy-start(f32[256,256]{1,0:T(8,128)} %online-softmax) | copy-start | bytes 786436
  86.5 7.8 %copy-start.13 = (f32[256,256]{1,0:T(8,128)S(1)}, f32[256,256]{1,0:T(8,128)}, u32[]{:S(2)}) copy-start(f32[256,256]{1,0:T(8,128)} %copy-done.12) | copy-start | bytes 786436
  86.5 7.8 %copy-start.32 = (bf16[256,256]{1,0:T(8,128)(2,1)S(1)}, bf16[256,256]{1,0:T(8,128)(2,1)}, u32[]{:S(2)}) copy-start(bf16[256,256]{1,0:T(8,128)(2,1)} %fusion.16) | copy-start | bytes 393220
  90.4 6.5 %collective-permute-start.4 = (bf16[256,256]{1,0:T(8,128)(2,1)S(1)}, bf16[256,256]{1,0:T(8,128)(2,1)S(1)}, u32[]{:S(2)}, u32[]{:S(2)}) collective-permute-start(bf16[256,256]{1,0:T(8,128)(2,1)S(1)} %convert_element_type.82), channel_id=1, source_target_pairs={{0,16},{16,0},{1,17},{17,1},{2,18},{18,2},{3,19},{19,3},{4,20},{20... | collective-permute-start | bytes 393224 | tf_op jit(solution)/shard_map/ppermute | solution.py:484
  92.2 8.5 %collective-permute-start.6 = (bf16[256,256]{1,0:T(8,128)(2,1)S(1)}, bf16[256,256]{1,0:T(8,128)(2,1)S(1)}, u32[]{:S(2)}, u32[]{:S(2)}) collective-permute-start(bf16[256,256]{1,0:T(8,128)(2,1)S(1)} %convolution_convert_fusion.8), channel_id=1, source_target_pairs={{0,16},{16,0},{1,17},{17,1},{2,18},{18,2},{3,19},{19,3},{4,20},{20... | collective-permute-start | bytes 393224 | tf_op jit(solution)/shard_map/ppermute | solution.py:484
  92.5 66.8 %collective-permute-start.7 = (bf16[256,256]{1,0:T(8,128)(2,1)S(1)}, bf16[256,256]{1,0:T(8,128)(2,1)S(1)}, u32[]{:S(2)}, u32[]{:S(2)}) collective-permute-start(bf16[256,256]{1,0:T(8,128)(2,1)S(1)} %convolution_convert_fusion.7), channel_id=1, source_target_pairs={{0,16},{16,0},{1,17},{17,1},{2,18},{18,2},{3,19},{19,3},{4,20},{20... | collective-permute-start | bytes 393224 | tf_op jit(solution)/shard_map/ppermute | solution.py:484
  94.6 11.4 %collective-permute-start.8 = (bf16[256,256]{1,0:T(8,128)(2,1)S(1)}, bf16[256,256]{1,0:T(8,128)(2,1)S(1)}, u32[]{:S(2)}, u32[]{:S(2)}) collective-permute-start(bf16[256,256]{1,0:T(8,128)(2,1)S(1)} %convolution_convert_fusion.6), channel_id=1, source_target_pairs={{0,16},{16,0},{1,17},{17,1},{2,18},{18,2},{3,19},{19,3},{4,20},{20... | collective-permute-start | bytes 393224 | tf_op jit(solution)/shard_map/ppermute | solution.py:484
  99.0 1.7 copy-start.20
  100.7 1.9 copy-start.2
  102.6 1.6 copy-start.17
  104.2 1.8 copy-start.22
  106.0 2.7 copy-start.15
  159.4 3.5 %copy-start.11 = (f32[512,2048]{1,0:T(8,128)S(1)}, f32[512,2048]{1,0:T(8,128)}, u32[]{:S(2)}) copy-start(f32[512,2048]{1,0:T(8,128)} %fusion.21) | copy-start | bytes 12582916
  159.4 3.5 %copy-start.24 = (bf16[2048,256]{1,0:T(8,128)(2,1)S(1)}, bf16[2048,256]{1,0:T(8,128)(2,1)}, u32[]{:S(2)}) copy-start(bf16[2048,256]{1,0:T(8,128)(2,1)} %param.12) | copy-start | bytes 3145732
  162.9 2.1 copy-start.3
  165.0 135.9 %copy-start.9 = (bf16[1,256,256]{2,1,0:T(8,128)(2,1)S(1)}, bf16[1,256,256]{2,1,0:T(8,128)(2,1)}, u32[]{:S(2)}) copy-start(bf16[1,256,256]{2,1,0:T(8,128)(2,1)} %param.9) | copy-start | bytes 393220
  165.0 135.9 %copy-start.25 = (bf16[1,256,256]{2,1,0:T(8,128)(2,1)S(1)}, bf16[1,256,256]{2,1,0:T(8,128)(2,1)}, u32[]{:S(2)}) copy-start(bf16[1,256,256]{2,1,0:T(8,128)(2,1)} %param.15) | copy-start | bytes 393220
  165.0 136.0 %copy-start.34 = (pred[256]{0:T(512)(128)(4,1)S(1)}, pred[256]{0:T(512)(128)(4,1)}, u32[]{:S(2)}) copy-start(pred[256]{0:T(512)(128)(4,1)} %copy-done.33) | copy-start | bytes 772

commit v2 on v1

--- a/solution.py
+++ b/solution.py
@@ -348,15 +348,32 @@
     )(dec, enc, cot)
 
 
-def scatter_kernel(po, ng, eg, out_o, out_n, out_e, *scratch):
+def line_peer(y, z, x, c, d):
+    return (y, ((z + d) % NZ) * 4 + x * 2 + c)
+
+
+def greet_all(place_here, peers):
+    barrier = pltpu.get_barrier_semaphore()
+    targets = [peers[way] for way in ("y", "x", "c")]
+    targets += [line_peer(*place_here, d) for d in range(1, NZ)]
+    for target in targets:
+        pl.semaphore_signal(barrier, inc=1, device_id=target, device_id_type=MESH)
+    pl.semaphore_wait(barrier, len(targets))
+
+
+def scatter_kernel(po, ng, eg, stat, out_o, out_n, out_e, out_s, *scratch):
     y, z, x, c, peers = place()
+    here = (y, z, x, c)
     sends = Sends()
+    stat_got, stat_sum, stat_sems = scratch[:3]
+    scratch = scratch[3:]
     tensors = []
     for t, (part, out, rows) in enumerate(((po, out_o, False), (ng, out_n, False), (eg, out_e, True))):
-        tensors.append((part, out, rows) + tuple(scratch[15 * t : 15 * t + 15]))
-
-    greet(z, peers)
-    for part, out, rows, rc, ax, rx, by, ry, v, su, ru, sd, rd, cs, xs, ys, us, ds in tensors:
+        tensors.append((part, out, rows) + tuple(scratch[12 * t : 12 * t + 12]))
+
+    greet_all(here, peers)
+    sends.start(None, stat, stat_got.at[0], stat_sems, 0, peers["c"])
+    for part, out, rows, rc, ax, rx, by, ry, v, sz, rz, cs, xs, ys, zs in tensors:
         block = row_block if rows else feature_block
         n = 4 if rows else 2
         for xx in (1 - x, x):
@@ -366,7 +383,7 @@
                     sends.start(None, block(part, s, j, xx, 1 - c), rc.at[at], cs, at, peers["c"])
 
     def across_x(tensor):
-        part, out, rows, rc, ax, rx, by, ry, v, su, ru, sd, rd, cs, xs, ys, us, ds = tensor
+        part, out, rows, rc, ax, rx, by, ry, v, sz, rz, cs, xs, ys, zs = tensor
         block = row_block if rows else feature_block
         n = 4 if rows else 2
         for s in (1 - y, y):
@@ -378,17 +395,18 @@
                 sends.start(None, ax.at[s * n + j], rx.at[s * n + j], xs, s * n + j, peers["x"])
 
     def across_y(tensor):
-        part, out, rows, rc, ax, rx, by, ry, v, su, ru, sd, rd, cs, xs, ys, us, ds = tensor
+        part, out, rows, rc, ax, rx, by, ry, v, sz, rz, cs, xs, ys, zs = tensor
         block = row_block if rows else feature_block
         n = 4 if rows else 2
-        for s in (1 - y, y):
+        for theirs in (True, False):
+            s = 1 - y if theirs else y
             for j in range(n):
                 at = (s * n + j) * 2 + x
                 arrived(None, rc.at[at], cs, at, peers["c"])
                 arrived(None, rx.at[s * n + j], xs, s * n + j, peers["x"])
                 own = block(part, s, j, x, c)[...].astype(F32)
                 total = own + rc[at].astype(F32) + rx[s * n + j].astype(F32)
-                if s is not y:
+                if theirs:
                     by[j] = total.astype(BF16)
                     sends.start(None, by.at[j], ry.at[j], ys, j, peers["y"])
                 elif rows:
@@ -397,7 +415,7 @@
                     v[2 * y + j] = total
 
     def along_z(tensor):
-        part, out, rows, rc, ax, rx, by, ry, v, su, ru, sd, rd, cs, xs, ys, us, ds = tensor
+        part, out, rows, rc, ax, rx, by, ry, v, sz, rz, cs, xs, ys, zs = tensor
         n = 4 if rows else 2
         for j in range(n):
             arrived(None, ry.at[j], ys, j, peers["y"])
@@ -405,47 +423,58 @@
                 v[j, :, pl.ds(pl.multiple_of((1 - y) * 2048, 2048), 2048)] = ry[j].astype(F32)
             else:
                 v[2 * (1 - y) + j] = ry[j].astype(F32)
-        for k in range(NZ):
-            for at, buf, sbuf, sems, way, got, on in (
-                (NZ - 1 - k, ru, su, us, "up", (z > 0) & (z <= NZ - 1 - k), z < NZ - 1 - k),
-                (k, rd, sd, ds, "down", (z < NZ - 1) & (z >= k), z > k),
-            ):
-                if not (way == "up" and at == 0) and not (way == "down" and at == NZ - 1):
-                    arrived(got, buf.at[at], sems, at, peers["c"])
-                    more = got & on
-
-                    @pl.when(more)
-                    def _(at=at, buf=buf, sbuf=sbuf):
-                        sbuf[at] = (v[at] + buf[at].astype(F32)).astype(BF16)
-
-                    @pl.when(jnp.logical_and(on, jnp.logical_not(got)))
-                    def _(at=at, sbuf=sbuf):
-                        sbuf[at] = v[at].astype(BF16)
-
-                    sends.start(on, sbuf.at[at], buf.at[at], sems, at, peers[way])
-        out[...] = v[z]
-
-        @pl.when(z > 0)
-        def _():
-            out[...] += ru[z].astype(F32)
-
-        @pl.when(z < NZ - 1)
-        def _():
-            out[...] += rd[z].astype(F32)
-
+        for d in (2, 1, 3):
+            sz[d - 1] = v[(z + d) % NZ].astype(BF16)
+            sends.start(None, sz.at[d - 1], rz.at[d - 1], zs, d - 1, line_peer(*here, d))
+
+    def close(tensor):
+        part, out, rows, rc, ax, rx, by, ry, v, sz, rz, cs, xs, ys, zs = tensor
+        total = v[z]
+        for d in range(1, NZ):
+            arrived(None, rz.at[d - 1], zs, d - 1, peers["c"])
+            total += rz[d - 1].astype(F32)
+        out[...] = total
+
+    def stat_step(k, way):
+        arrived(None, stat_got.at[k], stat_sems, k, peers["c"])
+        held = stat[...] if k == 0 else stat_sum[k - 1]
+        stat_sum[k] = held + stat_got[k]
+        if way:
+            sends.start(None, stat_sum.at[k], stat_got.at[k + 1], stat_sems, k + 1, peers[way])
+
+    across_x(tensors[0])
+    stat_step(0, "x")
+    across_x(tensors[1])
+    across_x(tensors[2])
+    stat_step(1, "y")
+    across_y(tensors[0])
+    across_y(tensors[1])
+    stat_step(2, None)
+    for d in range(1, NZ):
+        sends.start(
+            None, stat_sum.at[2], stat_got.at[2 + d], stat_sems, 2 + d, line_peer(*here, d)
+        )
+    along_z(tensors[0])
+    across_y(tensors[2])
+    along_z(tensors[1])
+    along_z(tensors[2])
+    total = stat_sum[2]
+    for d in range(1, NZ):
+        arrived(None, stat_got.at[2 + d], stat_sems, 2 + d, peers["c"])
+        total += stat_got[2 + d]
+    out_s[...] = total
     for tensor in tensors:
-        across_x(tensor)
-    for i, tensor in enumerate(tensors):
-        across_y(tensor)
-        if i:
-            along_z(tensors[i - 1])
-    along_z(tensors[-1])
+        close(tensor)
     sends.finish()
 
 
-def scatter(po, ng, eg):
+def scatter(po, ng, eg, stat):
     vmem = pl.BlockSpec(memory_space=pltpu.VMEM)
-    scratch = []
+    scratch = [
+        pltpu.VMEM((6, 8, 128), F32),
+        pltpu.VMEM((3, 8, 128), F32),
+        pltpu.SemaphoreType.DMA((2, 6)),
+    ]
     for rows in (False, False, True):
         n = 4 if rows else 2
         r, w, wz = (16, 2048, 4096) if rows else (256, 256, 256)
@@ -457,23 +486,24 @@
             pltpu.VMEM((n, r, w), BF16),
             pltpu.VMEM((NZ, r, wz), F32),
         ]
-        scratch += [pltpu.VMEM((NZ, r, wz), BF16)] * 4
-        scratch += [pltpu.SemaphoreType.DMA((2, k)) for k in (4 * n, 2 * n, n, NZ, NZ)]
+        scratch += [pltpu.VMEM((NZ - 1, r, wz), BF16)] * 2
+        scratch += [pltpu.SemaphoreType.DMA((2, k)) for k in (4 * n, 2 * n, n, NZ - 1)]
     return pl.pallas_call(
         scatter_kernel,
         out_shape=(
             jax.ShapeDtypeStruct((256, 256), F32),
             jax.ShapeDtypeStruct((256, 256), F32),
             jax.ShapeDtypeStruct((16, 4096), F32),
+            jax.ShapeDtypeStruct((8, 128), F32),
         ),
-        in_specs=[vmem] * 3,
-        out_specs=(vmem,) * 3,
+        in_specs=[vmem] * 4,
+        out_specs=(vmem,) * 4,
         scratch_shapes=scratch,
         compiler_params=pltpu.CompilerParams(
             collective_id=1, has_side_effects=True, vmem_limit_bytes=48 * 2**20
         ),
         name="reduce_scatter",
-    )(po, ng, eg)
+    )(po, ng, eg, stat)
 
 
 def dot(a, b, dims):
@@ -553,8 +583,10 @@
     part_enc = (
         dot(k_both, key_weight, ((1,), (1,))) + dot(v_both, value_weight, ((1,), (1,)))
     ).astype(BF16).reshape(2, -1, half)
-    stats = lax.psum(jnp.sum(part_normed.astype(F32) * hidden, axis=-1), ("dp", "mp")) / width
-    out_sum, normed_grad, enc_sum = scatter(part_out, part_normed, part_enc)
+    stats = jnp.sum(part_normed.astype(F32) * hidden, axis=-1).reshape(4, 128)
+    stats = jnp.concatenate([stats, jnp.zeros_like(stats)], axis=0)
+    out_sum, normed_grad, enc_sum, stats = scatter(part_out, part_normed, part_enc, stats)
+    stats = stats[:4].reshape(2, tokens) / width
 
     rows = ((0,), (0,))
     query_grad = dot(normed, q_both, rows).astype(BF16)

time: 303 us -> 197 us (0.65)
  Pallas kernels: 181 us -> 120 us
  blocking collectives: 48.7 us -> 0 us
    pallas_call x1, Pallas kernels: 135 us -> 74.3 us  [scatter(): pl.pallas_call(scatter_kernel, out_shape=(jax.ShapeDtypeStruct((256, 256)...]
    psum x1 -> x0, blocking collectives: 48.7 us -> none  [fast(): lax.psum(jnp.sum(part_normed.astype(F32) * hidden, axis=-1), ('dp', 'mp'))]
    unnamed x70 -> x72, local copies, waits for them, and re-layouts: 12.9 us -> 14.3 us
  transfers between devices with their start and end apart: 9 -> 9, of which waited for: 3 -> 3; matrix products, arithmetic and copies ran while one was open for 9% -> 14% of each run, Pallas kernels for 0% -> 0%
where the time goes in v2:
time: 197 us; the launch traced here: 196 us
  Pallas kernels  120 us (61%)
  matrix products  24.6 us (12%)
  local copies, waits for them, and re-layouts  19.3 us (10%)
  other arithmetic  13.5 us (7%)
  starting transfers between devices  8.3 us (4%)
  waiting for transfers between devices  7.38 us (4%)
  between operations  2.52 us (1%)
    pallas_call x1, Pallas kernels, scatter(): pl.pallas_call(scatter_kernel, out_shape=(jax.ShapeDtypeStruct((256, 256)...  74.3 us
    pallas_call x1, Pallas kernels, gather(): pl.pallas_call(gather_kernel, out_shape=(out, out, out), in_specs=[vmem]...  43.6 us
    dot_general x17, matrix products, dot(): return lax.dot_general(a, b, (dims, ((), ())), preferred_element_type=F32)  24.6 us
    unnamed x72, local copies, waits for them, and re-layouts  14.3 us
    ppermute x9, starting transfers between devices, swap(): return lax.ppermute(a, 'dp', [(0, 1), (1, 0)])  8.3 us
    ppermute x9, waiting for transfers between devices, swap(): return lax.ppermute(a, 'dp', [(0, 1), (1, 0)])  7.38 us
  transfers between devices with their start and end apart: 9, of which 3 were waited for; matrix products, arithmetic and copies ran while one was open for 14% of the time, Pallas kernels for 0%

profile of v2, /device:TPU:14, one launch (start us, length us, event | category | flops | bytes accessed | tf_op | source)
XLA Modules:
  0.0 195.6 jit_solution(4599782461014801730)
XLA Ops:
  1.4 1.0 bitcast_select_fusion.cot
  2.4 0.9 copy-done.8
  3.3 0.9 copy-done.12
  4.2 43.6 %gather_activations.1 = (bf16[3,256,2048]{2,1,0:T(8,128)(2,1)S(1)}, bf16[3,256,2048]{2,1,0:T(8,128)(2,1)S(1)}, bf16[3,256,2048]{2,1,0:T(8,128)(2,1)S(1)}) custom-call(bf16[256,256]{1,0:T(8,128)(2,1)S(1)} %bitcast.83, bf16[16,4096]{1,0:T(8,128)(2,1)S(1)} %bitcast.84, bf16[256,256]{1,0:T(8,128)(2,1)S(1)} %bitcast_select_fusion.cot), custom_call_target="tpu_custom_call" | custom-call | tf_op jit(solution)/shard_map/gather_activations/pallas_call | solution.py:338
  47.9 1.7 copy-done.4
  49.5 1.7 copy-done.7
  51.2 1.6 copy-done.1
  53.5 2.5 %fusion.4 = f32[2,256,256]{2,1,0:T(8,128)S(1)} fusion(bf16[3,256,2048]{2,1,0:T(8,128)(2,1)} %copy-done.7, bf16[256,2048]{1,0:T(8,128)(2,1)S(1)} %copy-done), kind=kOutput, calls=%fused_computation.18 | convolution fusion | flops 536870912 | bytes 4718592 | tf_op jit(solution)/shard_map/dot_general | solution.py:510
  56.0 0.8 dynamic-slice_bitcast_fusion
  56.8 2.0 %collective-permute-start.5 = (f32[256,256]{1,0:T(8,128)}, f32[256,256]{1,0:T(8,128)}, u32[]{:S(2)}, u32[]{:S(2)}) collective-permute-start(f32[256,256]{1,0:T(8,128)} %dynamic-slice_bitcast_fusion), channel_id=1, source_target_pairs={{0,16},{16,0},{1,17},{17,1},{2,18},{18,2},{3,19},{19,3},{4,20},{20... | collective-permute-start | bytes 786440 | tf_op jit(solution)/shard_map/ppermute | solution.py:514
  58.8 0.7 fusion.6
  59.5 0.7 copy-done.31
  60.3 0.7 fusion.8
  61.1 0.8 copy-done.29
  61.9 0.7 dynamic-slice_bitcast_fusion.2
  62.6 2.0 %collective-permute-start.2 = (f32[256,256]{1,0:T(8,128)}, f32[256,256]{1,0:T(8,128)}, u32[]{:S(2)}, u32[]{:S(2)}) collective-permute-start(f32[256,256]{1,0:T(8,128)} %dynamic-slice_bitcast_fusion.2), channel_id=1, source_target_pairs={{0,16},{16,0},{1,17},{17,1},{2,18},{18,2},{3,19},{19,3},{4,20},{20... | collective-permute-start | bytes 786440 | tf_op jit(solution)/shard_map/ppermute | solution.py:514
  65.2 1.9 slice.14
  67.7 1.5 slice.13
  69.3 2.1 %fusion.1 = bf16[2,256,2048]{2,1,0:T(8,128)(2,1)S(1)} fusion(f32[2,256]{1,0:T(2,128)S(1)} %add_rsqrt_fusion, bf16[3,256,2048]{2,1,0:T(8,128)(2,1)} %copy-done.1), kind=kLoop, calls=%fused_computation.4 | loop fusion | flops 3145728 | bytes 4196352 | tf_op jit(solution)/shard_map/convert_element_type | solution.py:543
  71.5 0.7 fusion.10
  72.9 1.6 fusion.16
  74.5 2.9 %collective-permute-done.2 = f32[256,256]{1,0:T(8,128)} collective-permute-done((f32[256,256]{1,0:T(8,128)}, f32[256,256]{1,0:T(8,128)}, u32[]{:S(2)}, u32[]{:S(2)}) %collective-permute-start.2) | collective-permute-done | bytes 262176 | tf_op jit(solution)/shard_map/ppermute | solution.py:514
  77.4 1.0 fusion.17
  78.4 1.7 bitcast_add_fusion.1
  80.1 2.5 %collective-permute-done.1 = f32[256,256]{1,0:T(8,128)S(1)} collective-permute-done((f32[256,256]{1,0:T(8,128)S(1)}, f32[256,256]{1,0:T(8,128)S(1)}, u32[]{:S(2)}, u32[]{:S(2)}) %collective-permute-start.1) | collective-permute-done | bytes 262176 | tf_op jit(solution)/shard_map/ppermute | solution.py:514
  84.3 2.1 %online-softmax = f32[256,256]{1,0:T(8,128)} custom-call(f32[256,256]{1,0:T(8,128)} %copy-done.14, f32[256,256]{1,0:T(8,128)} %bitcast_add_fusion.1), custom_call_target="tpu_custom_call" | custom-call | tf_op online-softmax
  86.5 1.5 multiply_reduce_fusion
  87.9 1.1 multiply_convert_fusion
  89.1 1.1 convolution_convert_fusion.7
  90.4 1.8 collective-permute-start.4
  92.5 1.7 collective-permute-start.7
  95.0 1.9 collective-permute-done.4
  96.9 2.1 %convolution_convert_fusion.1 = bf16[512,2048]{1,0:T(8,128)(2,1)} fusion(bf16[256,2048]{1,0:T(8,128)(2,1)S(1)} %copy-done, bf16[256,256]{1,0:T(8,128)(2,1)S(1)} %get-tuple-element.28, bf16[256,256]{1,0:T(8,128)(2,1)S(1)} %get-tuple-element.27), kind=kOutput, calls=%fused_computation.8 | convolution fusion | flops 538443776 | bytes 3407872 | tf_op jit(solution)/shard_map/dot_general | solution.py:510
  99.0 1.7 convolution_convert_fusion.2
  100.8 0.7 convolution_convert_fusion
  101.5 1.1 copy-done.2
  102.6 0.7 fusion.2
  103.3 0.9 copy-done.19
  104.2 1.7 convolution_convert_fusion.5
  106.0 2.7 %fusion.21 = f32[512,2048]{1,0:T(8,128)} fusion(bf16[2048,256]{1,0:T(8,128)(2,1)S(1)} %copy-done.24, bf16[256,256]{1,0:T(8,128)(2,1)S(1)} %get-tuple-element.24, bf16[256,256]{1,0:T(8,128)(2,1)S(1)} %get-tuple-element.23), kind=kOutput, calls=%fused_computation.52 | convolution fusion | flops 537395200 | bytes 5505024 | tf_op jit(solution)/shard_map/dot_general | solution.py:510
  108.7 1.9 convolution_convert_fusion.3
  110.7 3.5 %convolution_convert_fusion.4 = bf16[2048,256]{1,0:T(8,128)(2,1)} fusion(bf16[512,2048]{1,0:T(8,128)(2,1)} %bitcast.87, bf16[256,256]{1,0:T(8,128)(2,1)S(1)} %get-tuple-element.22, bf16[256,256]{1,0:T(8,128)(2,1)S(1)} %get-tuple-element.21), kind=kOutput, calls=%fused_computation.11 | convolution fusion | flops 537919488 | bytes 3407872 | tf_op jit(solution)/shard_map/dot_general | solution.py:510
  114.2 2.1 %add_convert_fusion = bf16[512,2048]{1,0:T(8,128)(2,1)} fusion(f32[512,2048]{1,0:T(8,128)S(1)} %copy-done.13, bf16[2048,256]{1,0:T(8,128)(2,1)S(1)} %copy-done.26, bf16[256,256]{1,0:T(8,128)(2,1)S(1)} %get-tuple-element.22, bf16[256,256]{1,0:T(8,128)(2,1)S(1)} %get-tuple-element.21), kind=kOutput, calls=%fused_computation.6 | convolution fusion | flops 539492352 | bytes 7602176 | tf_op jit(solution)/shard_map/dot_general | solution.py:510
  116.4 74.3 %reduce_scatter.1 = (f32[256,256]{1,0:T(8,128)S(1)}, f32[256,256]{1,0:T(8,128)S(1)}, f32[16,4096]{1,0:T(8,128)S(1)}, f32[8,128]{1,0:T(8,128)S(1)}) custom-call(bf16[2,256,2048]{2,1,0:T(8,128)(2,1)S(1)} %bitcast.82, bf16[2,256,2048]{2,1,0:T(8,128)(2,1)S(1)} %bitcast.81, bf16[2,256,2048]{2,1,0:T(8,128)(2,1)} %bitcast.86, f32[8,128]{1,0:T(8,128)S(1)} %concatenate.19.stat), custom_call_target="tpu_custom_call" | custom-call | tf_op jit(solution)/shard_map/reduce_scatter/pallas_call | solution.py:491
  190.7 0.7 copy-done.10
  191.4 0.7 copy-done.11
  192.1 1.6 convert_bitcast_fusion
  193.7 1.8 fusion.22
  (95 shorter events, 5.2 us)
Async XLA Ops:
  0.6 52.8 %copy-start = (bf16[256,2048]{1,0:T(8,128)(2,1)S(1)}, bf16[256,2048]{1,0:T(8,128)(2,1)}, u32[]{:S(2)}) copy-start(bf16[256,2048]{1,0:T(8,128)(2,1)} %param.14) | copy-start | bytes 3145732
  1.4 1.0 copy-start.34
  2.4 0.9 copy-start.8
  3.3 0.9 copy-start.12
  47.8 1.7 copy-start.4
  49.5 1.7 copy-start.7
  51.2 1.6 copy-start.1
  53.4 15.9 %collective-permute-start = (f32[2,256]{1,0:T(2,128)S(1)}, f32[2,256]{1,0:T(2,128)S(1)}, u32[]{:S(2)}, u32[]{:S(2)}) collective-permute-start(f32[2,256]{1,0:T(2,128)S(1)} %fusion), channel_id=1, source_target_pairs={{0,16},{16,0},{1,17},{17,1},{2,18},{18,2},{3,19},{19,3},{4,20},{20... | collective-permute-start | bytes 6152 | tf_op jit(solution)/shard_map/ppermute | solution.py:514
  53.4 5.3 %copy-start.5 = (bf16[3,256,2048]{2,1,0:T(8,128)(2,1)S(1)}, bf16[3,256,2048]{2,1,0:T(8,128)(2,1)}, u32[]{:S(2)}) copy-start(bf16[3,256,2048]{2,1,0:T(8,128)(2,1)} %copy-done.4) | copy-start | bytes 9437188
  53.5 5.3 %copy-start.23 = (bf16[2048,256]{1,0:T(8,128)(2,1)S(1)}, bf16[2048,256]{1,0:T(8,128)(2,1)}, u32[]{:S(2)}) copy-start(bf16[2048,256]{1,0:T(8,128)(2,1)} %param.13) | copy-start | bytes 3145732
  56.0 3.5 %copy-start.27 = (f32[2,256,256]{2,1,0:T(8,128)}, f32[2,256,256]{2,1,0:T(8,128)S(1)}, u32[]{:S(2)}) copy-start(f32[2,256,256]{2,1,0:T(8,128)S(1)} %fusion.4) | copy-start | bytes 1572868
  56.8 16.0 %collective-permute-start.5 = (f32[256,256]{1,0:T(8,128)}, f32[256,256]{1,0:T(8,128)}, u32[]{:S(2)}, u32[]{:S(2)}) collective-permute-start(f32[256,256]{1,0:T(8,128)} %dynamic-slice_bitcast_fusion), channel_id=1, source_target_pairs={{0,16},{16,0},{1,17},{17,1},{2,18},{18,2},{3,19},{19,3},{4,20},{20... | collective-permute-start | bytes 786440 | tf_op jit(solution)/shard_map/ppermute | solution.py:514
  58.8 1.6 copy-start.25
  59.5 0.8 copy-start.31
  60.3 18.1 %collective-permute-start.3 = (f32[256,256]{1,0:T(8,128)S(1)}, f32[256,256]{1,0:T(8,128)}, u32[]{:S(2)}, u32[]{:S(2)}) collective-permute-start(f32[256,256]{1,0:T(8,128)S(1)} %dynamic-slice_bitcast_fusion.1), channel_id=1, source_target_pairs={{0,16},{16,0},{1,17},{17,1},{2,18},{18,2},{3,19},{19,3},{4,20},{20... | collective-permute-start | bytes 786440 | tf_op jit(solution)/shard_map/ppermute | solution.py:514
  61.1 0.8 copy-start.29
  62.6 14.8 %collective-permute-start.2 = (f32[256,256]{1,0:T(8,128)}, f32[256,256]{1,0:T(8,128)}, u32[]{:S(2)}, u32[]{:S(2)}) collective-permute-start(f32[256,256]{1,0:T(8,128)} %dynamic-slice_bitcast_fusion.2), channel_id=1, source_target_pairs={{0,16},{16,0},{1,17},{17,1},{2,18},{18,2},{3,19},{19,3},{4,20},{20... | collective-permute-start | bytes 786440 | tf_op jit(solution)/shard_map/ppermute | solution.py:514
  65.2 2.5 %copy-start.6 = (bf16[3,256,2048]{2,1,0:T(8,128)(2,1)S(1)}, bf16[3,256,2048]{2,1,0:T(8,128)(2,1)}, u32[]{:S(2)}) copy-start(bf16[3,256,2048]{2,1,0:T(8,128)(2,1)} %copy-done.4) | copy-start | bytes 9437188
  69.3 2.1 %copy-start.21 = (bf16[2048,256]{1,0:T(8,128)(2,1)S(1)}, bf16[2048,256]{1,0:T(8,128)(2,1)}, u32[]{:S(2)}) copy-start(bf16[2048,256]{1,0:T(8,128)(2,1)} %param.11) | copy-start | bytes 3145732
  71.4 1.4 copy-start.18
  71.4 1.4 copy-start.28
  71.4 6.0 %copy-start.30 = (f32[2,256,256]{2,1,0:T(8,128)S(1)}, f32[2,256,256]{2,1,0:T(8,128)}, u32[]{:S(2)}) copy-start(f32[2,256,256]{2,1,0:T(8,128)} %copy-done.29) | copy-start | bytes 1572868
  71.4 7.0 %copy-start.32 = (f32[2,256,256]{2,1,0:T(8,128)S(1)}, f32[2,256,256]{2,1,0:T(8,128)}, u32[]{:S(2)}) copy-start(f32[2,256,256]{2,1,0:T(8,128)} %copy-done.31) | copy-start | bytes 1572868
  72.8 9.9 %collective-permute-start.1 = (f32[256,256]{1,0:T(8,128)S(1)}, f32[256,256]{1,0:T(8,128)S(1)}, u32[]{:S(2)}, u32[]{:S(2)}) collective-permute-start(f32[256,256]{1,0:T(8,128)S(1)} %dynamic-slice_bitcast_fusion.3), channel_id=1, source_target_pairs={{0,16},{16,0},{1,17},{17,1},{2,18},{18,2},{3,19},{19,3},{4,20},{20... | collective-permute-start | bytes 786440 | tf_op jit(solution)/shard_map/ppermute | solution.py:514
  82.7 0.7 copy-start.20
  83.6 0.7 copy-start.14
  86.4 3.9 %copy-start.16 = (f32[256,256]{1,0:T(8,128)S(1)}, f32[256,256]{1,0:T(8,128)}, u32[]{:S(2)}) copy-start(f32[256,256]{1,0:T(8,128)} %online-softmax) | copy-start | bytes 786436
  86.4 7.8 %copy-start.15 = (f32[256,256]{1,0:T(8,128)S(1)}, f32[256,256]{1,0:T(8,128)}, u32[]{:S(2)}) copy-start(f32[256,256]{1,0:T(8,128)} %copy-done.14) | copy-start | bytes 786436
  86.5 7.8 %copy-start.33 = (bf16[256,256]{1,0:T(8,128)(2,1)S(1)}, bf16[256,256]{1,0:T(8,128)(2,1)}, u32[]{:S(2)}) copy-start(bf16[256,256]{1,0:T(8,128)(2,1)} %fusion.16) | copy-start | bytes 393220
  90.4 6.5 %collective-permute-start.4 = (bf16[256,256]{1,0:T(8,128)(2,1)S(1)}, bf16[256,256]{1,0:T(8,128)(2,1)S(1)}, u32[]{:S(2)}, u32[]{:S(2)}) collective-permute-start(bf16[256,256]{1,0:T(8,128)(2,1)S(1)} %convert_element_type.82), channel_id=1, source_target_pairs={{0,16},{16,0},{1,17},{17,1},{2,18},{18,2},{3,19},{19,3},{4,20},{20... | collective-permute-start | bytes 393224 | tf_op jit(solution)/shard_map/ppermute | solution.py:514
  92.2 8.6 %collective-permute-start.6 = (bf16[256,256]{1,0:T(8,128)(2,1)S(1)}, bf16[256,256]{1,0:T(8,128)(2,1)S(1)}, u32[]{:S(2)}, u32[]{:S(2)}) collective-permute-start(bf16[256,256]{1,0:T(8,128)(2,1)S(1)} %convolution_convert_fusion.8), channel_id=1, source_target_pairs={{0,16},{16,0},{1,17},{17,1},{2,18},{18,2},{3,19},{19,3},{4,20},{20... | collective-permute-start | bytes 393224 | tf_op jit(solution)/shard_map/ppermute | solution.py:514
  92.5 18.2 %collective-permute-start.7 = (bf16[256,256]{1,0:T(8,128)(2,1)S(1)}, bf16[256,256]{1,0:T(8,128)(2,1)S(1)}, u32[]{:S(2)}, u32[]{:S(2)}) collective-permute-start(bf16[256,256]{1,0:T(8,128)(2,1)S(1)} %convolution_convert_fusion.7), channel_id=1, source_target_pairs={{0,16},{16,0},{1,17},{17,1},{2,18},{18,2},{3,19},{19,3},{4,20},{20... | collective-permute-start | bytes 393224 | tf_op jit(solution)/shard_map/ppermute | solution.py:514
  94.6 11.4 %collective-permute-start.8 = (bf16[256,256]{1,0:T(8,128)(2,1)S(1)}, bf16[256,256]{1,0:T(8,128)(2,1)S(1)}, u32[]{:S(2)}, u32[]{:S(2)}) collective-permute-start(bf16[256,256]{1,0:T(8,128)(2,1)S(1)} %convolution_convert_fusion.6), channel_id=1, source_target_pairs={{0,16},{16,0},{1,17},{17,1},{2,18},{18,2},{3,19},{19,3},{4,20},{20... | collective-permute-start | bytes 393224 | tf_op jit(solution)/shard_map/ppermute | solution.py:514
  99.0 1.7 copy-start.22
  100.7 1.9 copy-start.2
  102.6 1.6 copy-start.19
  104.2 1.8 copy-start.24
  106.0 2.7 %copy-start.17 = (bf16[2,256,2048]{2,1,0:T(8,128)(2,1)S(1)}, bf16[2,256,2048]{2,1,0:T(8,128)(2,1)}, u32[]{:S(2)}) copy-start(bf16[2,256,2048]{2,1,0:T(8,128)(2,1)} %slice.13) | copy-start | bytes 6291460
  110.7 3.5 %copy-start.13 = (f32[512,2048]{1,0:T(8,128)S(1)}, f32[512,2048]{1,0:T(8,128)}, u32[]{:S(2)}) copy-start(f32[512,2048]{1,0:T(8,128)} %fusion.21) | copy-start | bytes 12582916
  110.7 3.5 %copy-start.26 = (bf16[2048,256]{1,0:T(8,128)(2,1)S(1)}, bf16[2048,256]{1,0:T(8,128)(2,1)}, u32[]{:S(2)}) copy-start(bf16[2048,256]{1,0:T(8,128)(2,1)} %param.12) | copy-start | bytes 3145732
  114.2 2.1 %copy-start.3 = (bf16[512,2048]{1,0:T(8,128)(2,1)S(1)}, bf16[512,2048]{1,0:T(8,128)(2,1)}, u32[]{:S(2)}) copy-start(bf16[512,2048]{1,0:T(8,128)(2,1)} %convolution_convert_fusion.1) | copy-start | bytes 6291460
  116.4 77.4 %copy-start.9 = (bf16[1,256,256]{2,1,0:T(8,128)(2,1)S(1)}, bf16[1,256,256]{2,1,0:T(8,128)(2,1)}, u32[]{:S(2)}) copy-start(bf16[1,256,256]{2,1,0:T(8,128)(2,1)} %param.9) | copy-start | bytes 393220
  116.4 77.4 %copy-start.35 = (pred[256]{0:T(512)(128)(4,1)S(1)}, pred[256]{0:T(512)(128)(4,1)}, u32[]{:S(2)}) copy-start(pred[256]{0:T(512)(128)(4,1)} %copy-done.34) | copy-start | bytes 772
  190.7 0.7 copy-start.10
  191.4 0.7 copy-start.11

commit v3 on v0

--- a/solution.py
+++ b/solution.py
@@ -1,9 +1,16 @@
+import functools
+
 import jax
 import jax.numpy as jnp
 from jax import lax
+from jax.experimental import pallas as pl
+from jax.experimental.pallas import tpu as pltpu
 from jax.sharding import PartitionSpec as P
 
 DH = 256
+MESH = pl.DeviceIdType.MESH
+F32 = jnp.float32
+BF16 = jnp.bfloat16
 
 
 def local(
@@ -127,6 +134,564 @@
     return (layer_out, input_grad, enc_grad, query_grad, key_grad, value_grad, output_grad)
 
 
+NZ = 4
+
+
+def place():
+    y, m = lax.axis_index("dp"), lax.axis_index("mp")
+    z, x, c = m // 4, (m // 2) % 2, m % 2
+    peers = {
+        "up": (y, m + 4),
+        "down": (y, m - 4),
+        "y": (1 - y, m),
+        "x": (y, m + 2 - 4 * x),
+        "c": (y, m + 1 - 2 * c),
+    }
+    return y, z, x, c, peers
+
+
+def when(pred, act):
+    if pred is None:
+        act()
+    else:
+        pl.when(pred)(act)
+
+
+def both(a, b):
+    return b if a is None else a if b is None else jnp.logical_and(a, b)
+
+
+class Sends:
+    def __init__(self):
+        self.open = []
+
+    def start(self, pred, src, dst, sems, at, peer):
+        copy = pltpu.make_async_remote_copy(
+            src_ref=src,
+            dst_ref=dst,
+            send_sem=sems.at[0, at],
+            recv_sem=sems.at[1, at],
+            device_id=peer,
+            device_id_type=MESH,
+        )
+        when(pred, lambda: copy.start())
+        self.open.append((pred, copy))
+
+    def finish(self):
+        for pred, copy in self.open:
+            when(pred, lambda copy=copy: copy.wait_send())
+
+
+def arrived(pred, dst, sems, at, peer):
+    copy = pltpu.make_async_remote_copy(
+        src_ref=dst,
+        dst_ref=dst,
+        send_sem=sems.at[0, at],
+        recv_sem=sems.at[1, at],
+        device_id=peer,
+        device_id_type=MESH,
+    )
+    when(pred, lambda: copy.wait_recv())
+
+
+def feature_block(ref, s, j, x, c):
+    return ref.at[s, :, pl.ds(pl.multiple_of(j * 1024 + x * 512 + c * 256, 256), 256)]
+
+
+def row_block(ref, s, j, x, c):
+    return ref.at[s, pl.ds(pl.multiple_of(j * 64 + x * 32 + c * 16, 16), 16), :]
+
+
+def line_peer(y, z, x, c, d):
+    return (y, ((z + d) % NZ) * 4 + x * 2 + c)
+
+
+def greet(here, peers):
+    barrier = pltpu.get_barrier_semaphore()
+    targets = [peers[way] for way in ("y", "x", "c")]
+    targets += [line_peer(*here, d) for d in range(1, NZ)]
+    for target in targets:
+        pl.semaphore_signal(barrier, inc=1, device_id=target, device_id_type=MESH)
+    pl.semaphore_wait(barrier, len(targets))
+
+
+def matmul(a, b, dims=((1,), (0,))):
+    return lax.dot_general(a, b, (dims, ((), ())), preferred_element_type=F32)
+
+
+BY_ROWS = ((1,), (1,))
+BY_TOKENS = ((0,), (0,))
+
+
+def chunk(i, size):
+    return pl.ds(pl.multiple_of(i * size, size), size)
+
+
+def diagonal():
+    return lax.broadcasted_iota(jnp.int32, (256, 256), 0) == lax.broadcasted_iota(
+        jnp.int32, (256, 256), 1
+    )
+
+
+def to_row(column):
+    return jnp.sum(jnp.where(diagonal(), column, 0.0), axis=0, keepdims=True)
+
+
+def to_column(row):
+    return jnp.sum(jnp.where(diagonal(), row, 0.0), axis=1, keepdims=True)
+
+
+def two_rows(first, second):
+    upper = lax.broadcasted_iota(jnp.int32, (8, 256), 0) < 4
+    return jnp.where(upper, first, second)
+
+
+GATHER_SEMS, REDUCE_REFS = 5, 12
+
+
+def kernel(
+    enc_len, dec_len, dec, enc, cot, wq_hbm, wk_hbm, wv_hbm, wo_hbm,
+    layer_out, input_grad, enc_grad, query_grad, key_grad, value_grad, output_grad,
+    masked_own, gd, ge, gc, wq, wk, wv, wo, normed, column, inverse,
+    parts, parts_got, grads, po, ng, eg, squares, squares_got, stat,
+    stat_got, stat_sum, stat_sems, swap_sems, local_sems, *scratch,
+):
+    y, z, x, c, peers = place()
+    here = (y, z, x, c)
+    sends = Sends()
+
+    loads = []
+    for i, (src, dst) in enumerate(((wk_hbm, wk), (wv_hbm, wv), (wq_hbm, wq), (wo_hbm, wo))):
+        copy = pltpu.make_async_copy(src, dst, local_sems.at[i])
+        copy.start()
+        loads.append(copy)
+    token = lax.broadcasted_iota(jnp.int32, (256, 256), 0)
+    masked_own[...] = jnp.where(token < dec_len[0], cot[...].astype(F32), 0.0).astype(BF16)
+
+    gathers = []
+    for t, (own, out, rows) in enumerate(((enc, ge, True), (dec, gd, False), (masked_own, gc, False))):
+        gathers.append((t, own, out, rows) + tuple(scratch[GATHER_SEMS * t : GATHER_SEMS * (t + 1)]))
+    scratch = scratch[3 * GATHER_SEMS :]
+    local = [[], [], []]
+
+    def held(tensor, zz):
+        _, own, out, rows = tensor[:4]
+        if rows:
+            return [row_block(out, y, zz, x, c), row_block(out, 2, zz, x, c)]
+        slot = y + (2 - y) * ((zz // 2 + y) % 2)
+        return [feature_block(out, slot, zz % 2, x, c)]
+
+    def onward(tensor, zz, pred, own=None):
+        t, _, out, rows, up, down, ys, xs, cs = tensor
+        if rows:
+            mine = row_block(out, y, zz, x, c)
+            far = row_block(out, 2, zz, x, c)
+            src, src_far = (mine, far) if own is None else own
+            sends.start(pred, src_far, mine, ys, zz, peers["y"])
+            sends.start(pred, src, mine, xs, y * 4 + zz, peers["x"])
+            sends.start(pred, src, mine, cs, (y * 4 + zz) * 2 + x, peers["c"])
+            return
+        other = (zz // 2 + y) % 2
+        j = zz % 2
+        slot = y + (2 - y) * other
+        src = feature_block(out, slot, j, x, c) if own is None else own[0]
+        mine = feature_block(out, y, j, x, c)
+        sends.start(both(pred, other == 1), src, mine, ys, j, peers["y"])
+        near = both(pred, other == 0)
+        sends.start(near, src, mine, xs, y * 2 + j, peers["x"])
+        sends.start(near, src, mine, cs, (y * 2 + j) * 2 + x, peers["c"])
+
+    def gather_start(tensor):
+        t, own, out, rows, up, down = tensor[:6]
+        views = held(tensor, z)
+        srcs = [own]
+        if rows:
+            srcs = [own.at[:, chunk(y, 2048)], own.at[:, chunk(1 - y, 2048)]]
+        for i, (src, view) in enumerate(zip(srcs, views)):
+            sends.start(z < NZ - 1, src, view, up, i, peers["up"])
+            sends.start(z > 0, src, view, down, i, peers["down"])
+        onward(tensor, z, None, srcs)
+        for i, (src, view) in enumerate(zip(srcs, views)):
+            copy = pltpu.make_async_copy(src, view, local_sems.at[4 + 2 * t + i])
+            copy.start()
+            local[t].append(copy)
+
+    def gather_z(tensor):
+        t, own, out, rows, up, down = tensor[:6]
+        for k in range(NZ - 1):
+            below, above = z - 1 - k, z + 1 + k
+            for zz, ok, sems_way, way, more in (
+                (jnp.maximum(below, 0), below >= 0, up, "up", z < NZ - 1),
+                (jnp.minimum(above, NZ - 1), above < NZ, down, "down", z > 0),
+            ):
+                views = held(tensor, zz)
+                n = len(views)
+                for i, view in enumerate(views):
+                    arrived(ok, view, sems_way, k * n + i, peers["c"])
+                    if k + 1 < NZ - 1:
+                        sends.start(both(ok, more), view, view, sems_way, (k + 1) * n + i, peers[way])
+                onward(tensor, zz, ok)
+
+    def gather_y(tensor):
+        t, own, out, rows, up, down, ys, xs, cs = tensor
+        block, n = (row_block, 4) if rows else (feature_block, 2)
+        for j in range(n):
+            view = block(out, 1 - y, j, x, c)
+            arrived(None, view, ys, j, peers["y"])
+            sends.start(None, view, view, xs, (1 - y) * n + j, peers["x"])
+            sends.start(None, view, view, cs, ((1 - y) * n + j) * 2 + x, peers["c"])
+
+    def gather_x(tensor):
+        t, own, out, rows, up, down, ys, xs, cs = tensor
+        block, n = (row_block, 4) if rows else (feature_block, 2)
+        for s in (y, 1 - y):
+            for j in range(n):
+                view = block(out, s, j, 1 - x, c)
+                arrived(None, view, xs, s * n + j, peers["x"])
+                sends.start(None, view, view, cs, (s * n + j) * 2 + 1 - x, peers["c"])
+
+    def gather_c(tensor):
+        t, own, out, rows, up, down, ys, xs, cs = tensor
+        block, n = (row_block, 4) if rows else (feature_block, 2)
+        for s in range(2):
+            for j in range(n):
+                for xx in range(2):
+                    arrived(None, block(out, s, j, xx, 1 - c), cs, (s * n + j) * 2 + xx, peers["c"])
+        for copy in local[t]:
+            copy.wait()
+
+    def project(i, left, weight, dims=((1,), (0,))):
+        for s in (1 - y, y):
+            parts[i, s] = matmul(left[s], weight[...], dims)
+            if s is not y:
+                sends.start(None, parts.at[i, s], parts_got.at[i], swap_sems, i, peers["y"])
+
+    def projected(i):
+        arrived(None, parts_got.at[i], swap_sems, i, peers["y"])
+        return (parts[i, y] + parts_got[i]).astype(BF16)
+
+    greet(here, peers)
+    e, d, g = gathers
+    gather_start(e)
+    gather_start(d)
+    gather_z(e)
+    gather_start(g)
+    gather_y(e)
+    gather_z(d)
+    gather_x(e)
+    gather_y(d)
+    gather_z(g)
+    gather_c(e)
+    loads[0].wait()
+    project(0, ge, wk)
+    gather_x(d)
+    gather_y(g)
+    gather_c(d)
+
+    @pl.loop(0, 16)
+    def _(i):
+        s, rows = i // 8, chunk(i % 8, 32)
+        value = gd[s, rows, :].astype(F32)
+        total = jnp.sum(value * value, axis=-1, keepdims=True)
+        column[s, rows, :] = jnp.broadcast_to(total, (32, 128))
+
+    squares[...] = two_rows(to_row(column[0, :, 0:1]), to_row(column[1, :, 0:1]))
+    sends.start(None, squares, squares_got, swap_sems, 8, peers["y"])
+    loads[1].wait()
+    project(1, ge, wv)
+    arrived(None, squares_got, swap_sems, 8, peers["y"])
+    features = 16 * dec.shape[1]
+    inv_rows = lax.rsqrt((squares[...] + squares_got[...]) / features + 1e-06)
+    for s in range(2):
+        inverse[s] = jnp.broadcast_to(to_column(inv_rows[4 * s : 4 * s + 1]), (256, 128))
+
+    @pl.loop(0, 16)
+    def _(i):
+        s, rows = i // 8, chunk(i % 8, 32)
+        value = gd[s, rows, :].astype(F32) * inverse[s, rows, 0:1]
+        normed[s, rows, :] = value.astype(BF16)
+
+    loads[2].wait()
+    project(2, normed, wq)
+    gather_x(g)
+    gather_c(g)
+    loads[3].wait()
+    project(3, gc, wo, BY_ROWS)
+
+    scale = DH ** (-0.5)
+    keyed = projected(0)
+    query = projected(2)
+    scores = matmul(query, keyed, BY_ROWS) * scale
+    position = lax.broadcasted_iota(jnp.int32, (256, 256), 1)
+    scores = jnp.where(position < enc_len[0], scores, -1e30)
+    shifted = jnp.exp(scores - jnp.max(scores, axis=-1, keepdims=True))
+    probs = shifted / jnp.sum(shifted, axis=-1, keepdims=True)
+    probs_low = probs.astype(BF16)
+    valued = projected(1)
+
+    def share(i, value):
+        grads[i, y] = value.astype(BF16)
+        sends.start(None, grads.at[i, y], grads.at[i, y], swap_sems, 4 + i, peers["y"])
+
+    def shared(i):
+        arrived(None, grads.at[i, 1 - y], swap_sems, 4 + i, peers["y"])
+
+    ATT, QG, KG, VG = range(4)
+    share(ATT, matmul(probs_low, valued))
+    attended_grad = projected(3)
+    probs_grad = matmul(attended_grad, valued, BY_ROWS)
+    scores_grad = (
+        probs * (probs_grad - jnp.sum(probs * probs_grad, axis=-1, keepdims=True)) * scale
+    ).astype(BF16)
+    share(QG, matmul(scores_grad, keyed))
+    share(KG, matmul(scores_grad, query, BY_TOKENS))
+    share(VG, matmul(probs_low, attended_grad, BY_TOKENS))
+
+    reduces = []
+    for t, (part, rows) in enumerate(((po, False), (ng, False), (eg, True))):
+        reduces.append((part, rows) + tuple(scratch[REDUCE_REFS * t : REDUCE_REFS * (t + 1)]))
+
+    def across_core(tensor, s):
+        part, rows, rc, ax, rx, by, ry, v, sz, rz, cs, xs, ys, zs = tensor
+        block, n = (row_block, 4) if rows else (feature_block, 2)
+        for xx in (1 - x, x):
+            for j in range(n):
+                at = (s * n + j) * 2 + xx
+                sends.start(None, block(part, s, j, xx, 1 - c), rc.at[at], cs, at, peers["c"])
+
+    def across_x(tensor, s):
+        part, rows, rc, ax, rx, by, ry, v, sz, rz, cs, xs, ys, zs = tensor
+        block, n = (row_block, 4) if rows else (feature_block, 2)
+        for j in range(n):
+            at = (s * n + j) * 2 + 1 - x
+            arrived(None, rc.at[at], cs, at, peers["c"])
+            own = block(part, s, j, 1 - x, c)[...].astype(F32)
+            ax[s * n + j] = (own + rc[at].astype(F32)).astype(BF16)
+            sends.start(None, ax.at[s * n + j], rx.at[s * n + j], xs, s * n + j, peers["x"])
+
+    def across_y(tensor, theirs):
+        part, rows, rc, ax, rx, by, ry, v, sz, rz, cs, xs, ys, zs = tensor
+        block, n = (row_block, 4) if rows else (feature_block, 2)
+        s = 1 - y if theirs else y
+        for j in range(n):
+            at = (s * n + j) * 2 + x
+            arrived(None, rc.at[at], cs, at, peers["c"])
+            arrived(None, rx.at[s * n + j], xs, s * n + j, peers["x"])
+            own = block(part, s, j, x, c)[...].astype(F32)
+            total = own + rc[at].astype(F32) + rx[s * n + j].astype(F32)
+            if theirs:
+                by[j] = total.astype(BF16)
+                sends.start(None, by.at[j], ry.at[j], ys, j, peers["y"])
+            elif rows:
+                v[j, :, chunk(y, 2048)] = total
+            else:
+                v[2 * y + j] = total
+
+    def along_z(tensor):
+        part, rows, rc, ax, rx, by, ry, v, sz, rz, cs, xs, ys, zs = tensor
+        n = 4 if rows else 2
+        for j in range(n):
+            arrived(None, ry.at[j], ys, j, peers["y"])
+            if rows:
+                v[j, :, chunk(1 - y, 2048)] = ry[j].astype(F32)
+            else:
+                v[2 * (1 - y) + j] = ry[j].astype(F32)
+        for step in (2, 1, 3):
+            sz[step - 1] = v[(z + step) % NZ].astype(BF16)
+            sends.start(
+                None, sz.at[step - 1], rz.at[step - 1], zs, step - 1, line_peer(*here, step)
+            )
+
+    def summed(tensor):
+        part, rows, rc, ax, rx, by, ry, v, sz, rz, cs, xs, ys, zs = tensor
+        total = v[z]
+        for step in range(1, NZ):
+            arrived(None, rz.at[step - 1], zs, step - 1, peers["c"])
+            total += rz[step - 1].astype(F32)
+        return total
+
+    def stat_step(k, way):
+        arrived(None, stat_got.at[k], stat_sems, k, peers["c"])
+        before = stat[...] if k == 0 else stat_sum[k - 1]
+        stat_sum[k] = before + stat_got[k]
+        if way:
+            sends.start(None, stat_sum.at[k], stat_got.at[k + 1], stat_sems, k + 1, peers[way])
+
+    def out_parts(s):
+        @pl.loop(0, 4)
+        def _(i):
+            po[s, :, chunk(i, 512)] = matmul(grads[ATT, s], wo[:, chunk(i, 512)]).astype(BF16)
+
+    def normed_parts(s):
+        column[s] = jnp.zeros((256, 128), F32)
+
+        @pl.loop(0, 8)
+        def _(i):
+            cols = chunk(i, 256)
+            part = matmul(grads[QG, s], wq[cols, :], BY_ROWS).astype(BF16)
+            ng[s, :, cols] = part
+            dots = jnp.sum(part.astype(F32) * gd[s, :, cols].astype(F32), axis=-1, keepdims=True)
+            column[s] += jnp.broadcast_to(dots, (256, 128))
+
+    def enc_parts(s):
+        @pl.loop(0, 4)
+        def _(i):
+            cols = chunk(i, 512)
+            total = matmul(grads[KG, s], wk[cols, :], BY_ROWS)
+            total += matmul(grads[VG, s], wv[cols, :], BY_ROWS)
+            eg[s, :, cols] = total.astype(BF16)
+
+    def weight_part(out, left, i):
+        @pl.loop(0, 8)
+        def _(step):
+            rows = chunk(step, 256)
+            total = matmul(left[0, :, rows], grads[i, 0], BY_TOKENS)
+            total += matmul(left[1, :, rows], grads[i, 1], BY_TOKENS)
+            out[rows, :] = total.astype(BF16)
+
+    ro, rn, re = reduces
+    out_parts(y)
+    across_core(ro, y)
+    normed_parts(y)
+    across_core(rn, y)
+    across_x(ro, y)
+    shared(ATT)
+    out_parts(1 - y)
+    across_core(ro, 1 - y)
+    shared(QG)
+    across_x(rn, y)
+    normed_parts(1 - y)
+    across_core(rn, 1 - y)
+    across_x(ro, 1 - y)
+    stat[...] = two_rows(to_row(column[0, :, 0:1]), to_row(column[1, :, 0:1]))
+    sends.start(None, stat, stat_got.at[0], stat_sems, 0, peers["c"])
+    shared(KG)
+    shared(VG)
+    enc_parts(1 - y)
+    across_core(re, 1 - y)
+    across_x(rn, 1 - y)
+    enc_parts(y)
+    across_core(re, y)
+    stat_step(0, "x")
+    across_x(re, 1 - y)
+    across_x(re, y)
+    weight_part(query_grad, normed, QG)
+    across_y(ro, True)
+    across_y(ro, False)
+    stat_step(1, "y")
+    weight_part(key_grad, ge, KG)
+    along_z(ro)
+    across_y(rn, True)
+    across_y(rn, False)
+    stat_step(2, None)
+    for step in range(1, NZ):
+        sends.start(
+            None, stat_sum.at[2], stat_got.at[2 + step], stat_sems, 2 + step, line_peer(*here, step)
+        )
+    along_z(rn)
+    weight_part(value_grad, ge, VG)
+    across_y(re, True)
+    across_y(re, False)
+    along_z(re)
+
+    @pl.loop(0, 4)
+    def _(i):
+        cols = chunk(i, 512)
+        total = matmul(grads[ATT, 0], gc[0, :, cols], BY_TOKENS)
+        total += matmul(grads[ATT, 1], gc[1, :, cols], BY_TOKENS)
+        output_grad[:, cols] = total.astype(BF16)
+
+    layer_out[...] = (dec[...].astype(F32) + summed(ro)).astype(BF16)
+    total = stat_sum[2]
+    for step in range(1, NZ):
+        arrived(None, stat_got.at[2 + step], stat_sems, 2 + step, peers["c"])
+        total += stat_got[2 + step]
+    mean = to_column(jnp.where(y == 0, total[0:1], total[4:5])) / features
+    inv = inverse[y][:, 0:1]
+    input_grad[...] = (
+        masked_own[...].astype(F32)
+        + inv * summed(rn)
+        - dec[...].astype(F32) * (inv * inv * inv) * mean
+    ).astype(BF16)
+    enc_grad[...] = summed(re).astype(BF16)
+    sends.finish()
+
+
+def fast(
+    dec_input,
+    enc_output,
+    query_weight,
+    key_weight,
+    value_weight,
+    output_weight,
+    cotangent,
+    enc_lengths,
+    dec_lengths,
+):
+    vmem = pl.BlockSpec(memory_space=pltpu.VMEM)
+    smem = pl.BlockSpec(memory_space=pltpu.SMEM)
+    hbm = pl.BlockSpec(memory_space=pl.ANY)
+    dma = lambda *shape: pltpu.SemaphoreType.DMA(shape)
+    scratch = [
+        pltpu.VMEM((256, 256), BF16),
+        pltpu.VMEM((3, 256, 2048), BF16),
+        pltpu.VMEM((3, 256, 2048), BF16),
+        pltpu.VMEM((3, 256, 2048), BF16),
+        pltpu.VMEM((2048, 256), BF16),
+        pltpu.VMEM((2048, 256), BF16),
+        pltpu.VMEM((2048, 256), BF16),
+        pltpu.VMEM((256, 2048), BF16),
+        pltpu.VMEM((2, 256, 2048), BF16),
+        pltpu.VMEM((2, 256, 128), F32),
+        pltpu.VMEM((2, 256, 128), F32),
+        pltpu.VMEM((4, 2, 256, 256), F32),
+        pltpu.VMEM((4, 256, 256), F32),
+        pltpu.VMEM((4, 2, 256, 256), BF16),
+        pltpu.VMEM((2, 256, 2048), BF16),
+        pltpu.VMEM((2, 256, 2048), BF16),
+        pltpu.VMEM((2, 256, 2048), BF16),
+        pltpu.VMEM((8, 256), F32),
+        pltpu.VMEM((8, 256), F32),
+        pltpu.VMEM((8, 256), F32),
+        pltpu.VMEM((6, 8, 256), F32),
+        pltpu.VMEM((3, 8, 256), F32),
+        dma(2, 6),
+        dma(2, 9),
+        dma(10),
+    ]
+    for n in (2, 1, 1):
+        scratch += [dma(2, count * n) for count in (3, 3, 2, 4, 8)]
+    for rows in (False, False, True):
+        n = 4 if rows else 2
+        r, w, wz = (16, 2048, 4096) if rows else (256, 256, 256)
+        scratch += [
+            pltpu.VMEM((4 * n, r, w), BF16),
+            pltpu.VMEM((2 * n, r, w), BF16),
+            pltpu.VMEM((2 * n, r, w), BF16),
+            pltpu.VMEM((n, r, w), BF16),
+            pltpu.VMEM((n, r, w), BF16),
+            pltpu.VMEM((NZ, r, wz), F32),
+        ]
+        scratch += [pltpu.VMEM((NZ - 1, r, wz), BF16)] * 2
+        scratch += [dma(2, k) for k in (4 * n, 2 * n, n, NZ - 1)]
+    shapes = ((256, 256), (256, 256), (16, 4096)) + ((2048, 256),) * 3 + ((256, 2048),)
+    results = pl.pallas_call(
+        kernel,
+        out_shape=tuple(jax.ShapeDtypeStruct(shape, BF16) for shape in shapes),
+        in_specs=[smem, smem, vmem, vmem, vmem, hbm, hbm, hbm, hbm],
+        out_specs=(vmem,) * 7,
+        scratch_shapes=scratch,
+        compiler_params=pltpu.CompilerParams(
+            collective_id=0, has_side_effects=True, vmem_limit_bytes=58 * 2**20
+        ),
+        name="cross_attention",
+    )(
+        enc_lengths, dec_lengths, dec_input[0], enc_output[0], cotangent[0],
+        query_weight, key_weight, value_weight, output_weight,
+    )
+    return tuple(out[None] for out in results[:3]) + tuple(results[3:])
+
+
 def solution(mesh):
     in_specs = (
         P("dp", None, "mp"),
@@ -148,4 +713,5 @@
         P("dp", "mp"),
         P("mp", "dp"),
     )
-    return jax.shard_map(local, mesh=mesh, in_specs=in_specs, out_specs=out_specs, check_vma=False)
+    program = fast if dict(mesh.shape) == {"dp": 2, "mp": 16} else local
+    return jax.shard_map(program, mesh=mesh, in_specs=in_specs, out_specs=out_specs, check_vma=False)

time: 620 us -> 144 us (0.23)
  waiting for transfers between devices: 549 us -> 0 us
  Pallas kernels: 0 us -> 132 us
  matrix products: 28 us -> 0 us
  other arithmetic: 15 us -> 0 us
  between operations: 15.4 us -> 1.95 us
    all_gather x7 -> x0, waiting for transfers between devices: 251 us -> none  [the longest x1 43.9 us: local(): upstream = lax.all_gather(cotangent, 'mp', axis=2, tiled=True)[0]]
    reduce_scatter x3 -> x0, waiting for transfers between devices: 218 us -> none  [the longest x1 98 us: local(): lax.psum_scatter(jnp.concatenate([jnp.dot(normed.T, q_grad, preferred_ele...]
    pallas_call x0 -> x1, Pallas kernels: none -> 132 us  [fast(): pl.pallas_call(kernel, out_shape=tuple((jax.ShapeDtypeStruct(shape, BF16)...]
    psum x1 -> x0, waiting for transfers between devices: 74.9 us -> none  [local(): lax.psum(normed_part.astype(jnp.bfloat16), 'mp').astype(jnp.float32)]
    dot_general x18 -> x0, matrix products: 28 us -> none  [the longest x1 3.66 us: local(): jnp.dot(attended, output_full, preferred_element_type=jnp.float32)]
  transfers between devices with their start and end apart: 11 -> 0, of which waited for: 11 -> 0; matrix products, arithmetic and copies ran while one was open for 7% -> 0% of each run, Pallas kernels for 0% -> 0%
where the time goes in v3:
time: 144 us; the launch traced here: 143 us
  Pallas kernels  132 us (92%)
  local copies, waits for them, and re-layouts  9.74 us (7%)
  between operations  1.95 us (1%)
    pallas_call x1, Pallas kernels, fast(): pl.pallas_call(kernel, out_shape=tuple((jax.ShapeDtypeStruct(shape, BF16)...  132 us
    unnamed x17, local copies, waits for them, and re-layouts  9.74 us

profile of v3, /device:TPU:14, one launch (start us, length us, event | category | flops | bytes accessed | tf_op | source)
XLA Modules:
  0.0 143.4 jit_solution(16217809805838435257)
XLA Ops:
  1.9 131.7 %cross_attention.1 = (bf16[256,256]{1,0:T(8,128)(2,1)}, bf16[256,256]{1,0:T(8,128)(2,1)}, bf16[16,4096]{1,0:T(8,128)(2,1)}, bf16[2048,256]{1,0:T(8,128)(2,1)}, b...) custom-call(s32[1]{0:T(128)S(6)} %copy.23.enc_len, s32[1]{0:T(128)S(6)} %copy.24.dec_len, ...), custom_call_target="tpu_custom_call" | custom-call | tf_op jit(solution)/shard_map/cross_attention/pallas_call | solution.py:678
  133.6 0.0 copy-start.4
  133.6 1.6 %copy.25 = bf16[1,256,256]{2,1,0:T(8,128)(2,1)} copy(bf16[1,256,256]{2,1,0:T(8,128)(2,1)} %bitcast.11) | data formatting | bytes 262144
  135.2 0.0 copy-done.4
  135.2 0.0 copy-start.3
  135.2 0.7 copy.26
  135.9 0.3 copy-done.3
  136.2 0.7 copy.27
  136.8 0.0 copy-start.2
  136.8 2.4 %copy.28 = bf16[2048,256]{1,0:T(8,128)(2,1)} copy(bf16[2048,256]{1,0:T(8,128)(2,1)} %get-tuple-element.31) | data formatting | bytes 2097152
  139.2 0.0 copy-done.2
  139.2 0.0 copy-start.1
  139.2 1.0 copy.29
  140.2 0.6 copy-done.1
  140.8 0.0 copy-start
  140.8 1.0 copy.30
  141.8 0.6 copy-done
  142.4 1.0 copy.31
Async XLA Ops:
  133.6 1.6 %copy-start.4 = (bf16[256,256]{1,0:T(8,128)(2,1)S(1)}, bf16[256,256]{1,0:T(8,128)(2,1)}, u32[]{:S(2)}) copy-start(bf16[256,256]{1,0:T(8,128)(2,1)} %get-tuple-element.15) | copy-start | bytes 393220
  135.2 1.0 copy-start.3
  136.8 2.4 %copy-start.2 = (bf16[2048,256]{1,0:T(8,128)(2,1)S(1)}, bf16[2048,256]{1,0:T(8,128)(2,1)}, u32[]{:S(2)}) copy-start(bf16[2048,256]{1,0:T(8,128)(2,1)} %get-tuple-element.32) | copy-start | bytes 3145732
  139.2 1.6 %copy-start.1 = (bf16[2048,256]{1,0:T(8,128)(2,1)S(1)}, bf16[2048,256]{1,0:T(8,128)(2,1)}, u32[]{:S(2)}) copy-start(bf16[2048,256]{1,0:T(8,128)(2,1)} %get-tuple-element.33) | copy-start | bytes 3145732
  140.8 1.6 %copy-start = (bf16[256,2048]{1,0:T(8,128)(2,1)S(1)}, bf16[256,2048]{1,0:T(8,128)(2,1)}, u32[]{:S(2)}) copy-start(bf16[256,2048]{1,0:T(8,128)(2,1)} %get-tuple-element.34) | copy-start | bytes 3145732

commit v4 on v3

--- a/solution.py
+++ b/solution.py
@@ -251,8 +251,8 @@
 
 def kernel(
     enc_len, dec_len, dec, enc, cot, wq_hbm, wk_hbm, wv_hbm, wo_hbm,
-    layer_out, input_grad, enc_grad, query_grad, key_grad, value_grad, output_grad,
-    masked_own, gd, ge, gc, wq, wk, wv, wo, normed, column, inverse,
+    layer_out, input_grad, enc_grad, query_out, key_out, value_out, output_out,
+    query_grad, key_grad, value_grad, output_grad, masked_own, gd, ge, gc, wq, wk, wv, wo, normed, column, inverse,
     parts, parts_got, grads, po, ng, eg, squares, squares_got, stat,
     stat_got, stat_sum, stat_sems, swap_sems, local_sems, *scratch,
 ):
@@ -414,9 +414,15 @@
     loads[2].wait()
     project(2, normed, wq)
     gather_x(g)
-    gather_c(g)
-    loads[3].wait()
-    project(3, gc, wo, BY_ROWS)
+
+    ATT, QG, KG, VG = range(4)
+
+    def share(i, value):
+        grads[i, y] = value.astype(BF16)
+        sends.start(None, grads.at[i, y], grads.at[i, y], swap_sems, 4 + i, peers["y"])
+
+    def shared(i):
+        arrived(None, grads.at[i, 1 - y], swap_sems, 4 + i, peers["y"])
 
     scale = DH ** (-0.5)
     keyed = projected(0)
@@ -428,24 +434,10 @@
     probs = shifted / jnp.sum(shifted, axis=-1, keepdims=True)
     probs_low = probs.astype(BF16)
     valued = projected(1)
-
-    def share(i, value):
-        grads[i, y] = value.astype(BF16)
-        sends.start(None, grads.at[i, y], grads.at[i, y], swap_sems, 4 + i, peers["y"])
-
-    def shared(i):
-        arrived(None, grads.at[i, 1 - y], swap_sems, 4 + i, peers["y"])
-
-    ATT, QG, KG, VG = range(4)
     share(ATT, matmul(probs_low, valued))
-    attended_grad = projected(3)
-    probs_grad = matmul(attended_grad, valued, BY_ROWS)
-    scores_grad = (
-        probs * (probs_grad - jnp.sum(probs * probs_grad, axis=-1, keepdims=True)) * scale
-    ).astype(BF16)
-    share(QG, matmul(scores_grad, keyed))
-    share(KG, matmul(scores_grad, query, BY_TOKENS))
-    share(VG, matmul(probs_low, attended_grad, BY_TOKENS))
+    gather_c(g)
+    loads[3].wait()
+    project(3, gc, wo, BY_ROWS)
 
     reduces = []
     for t, (part, rows) in enumerate(((po, False), (ng, False), (eg, True))):
@@ -517,6 +509,12 @@
         if way:
             sends.start(None, stat_sum.at[k], stat_got.at[k + 1], stat_sems, k + 1, peers[way])
 
+    def emit(i, value):
+        out = (output_out, query_out, key_out, value_out)[i]
+        copy = pltpu.make_async_copy(value, out, local_sems.at[10 + i])
+        copy.start()
+        loads.append(copy)
+
     def out_parts(s):
         @pl.loop(0, 4)
         def _(i):
@@ -549,38 +547,49 @@
             total += matmul(left[1, :, rows], grads[i, 1], BY_TOKENS)
             out[rows, :] = total.astype(BF16)
 
+        emit(i, out)
+
     ro, rn, re = reduces
     out_parts(y)
     across_core(ro, y)
-    normed_parts(y)
-    across_core(rn, y)
-    across_x(ro, y)
     shared(ATT)
     out_parts(1 - y)
     across_core(ro, 1 - y)
+    across_x(ro, y)
+    across_x(ro, 1 - y)
+
+    attended_grad = projected(3)
+    probs_grad = matmul(attended_grad, valued, BY_ROWS)
+    scores_grad = (
+        probs * (probs_grad - jnp.sum(probs * probs_grad, axis=-1, keepdims=True)) * scale
+    ).astype(BF16)
+    share(QG, matmul(scores_grad, keyed))
+    share(KG, matmul(scores_grad, query, BY_TOKENS))
+    share(VG, matmul(probs_low, attended_grad, BY_TOKENS))
+    normed_parts(y)
+    across_core(rn, y)
+    enc_parts(y)
+    across_core(re, y)
+    across_x(rn, y)
     shared(QG)
-    across_x(rn, y)
     normed_parts(1 - y)
     across_core(rn, 1 - y)
-    across_x(ro, 1 - y)
     stat[...] = two_rows(to_row(column[0, :, 0:1]), to_row(column[1, :, 0:1]))
     sends.start(None, stat, stat_got.at[0], stat_sems, 0, peers["c"])
+    across_x(re, y)
     shared(KG)
     shared(VG)
     enc_parts(1 - y)
     across_core(re, 1 - y)
     across_x(rn, 1 - y)
-    enc_parts(y)
-    across_core(re, y)
+    across_y(ro, True)
+    across_y(ro, False)
     stat_step(0, "x")
     across_x(re, 1 - y)
-    across_x(re, y)
+    along_z(ro)
     weight_part(query_grad, normed, QG)
-    across_y(ro, True)
-    across_y(ro, False)
     stat_step(1, "y")
     weight_part(key_grad, ge, KG)
-    along_z(ro)
     across_y(rn, True)
     across_y(rn, False)
     stat_step(2, None)
@@ -600,6 +609,8 @@
         total = matmul(grads[ATT, 0], gc[0, :, cols], BY_TOKENS)
         total += matmul(grads[ATT, 1], gc[1, :, cols], BY_TOKENS)
         output_grad[:, cols] = total.astype(BF16)
+
+    emit(ATT, output_grad)
 
     layer_out[...] = (dec[...].astype(F32) + summed(ro)).astype(BF16)
     total = stat_sum[2]
@@ -614,7 +625,32 @@
         - dec[...].astype(F32) * (inv * inv * inv) * mean
     ).astype(BF16)
     enc_grad[...] = summed(re).astype(BF16)
+    for copy in loads[4:]:
+        copy.wait()
     sends.finish()
+
+
+def write_kernel(*refs):
+    n = (len(refs) - 1) // 2
+    sems = refs[-1]
+    copies = [pltpu.make_async_copy(refs[i], refs[n + i], sems.at[i]) for i in range(n)]
+    for copy in copies:
+        copy.start()
+    for copy in copies:
+        copy.wait()
+
+
+def write_out(results):
+    hbm = pl.BlockSpec(memory_space=pl.ANY)
+    return pl.pallas_call(
+        write_kernel,
+        out_shape=tuple(jax.ShapeDtypeStruct(r.shape, r.dtype) for r in results),
+        in_specs=[hbm] * len(results),
+        out_specs=(hbm,) * len(results),
+        scratch_shapes=[pltpu.SemaphoreType.DMA((len(results),))],
+        compiler_params=pltpu.CompilerParams(vmem_limit_bytes=60 * 2**20),
+        name="write_out",
+    )(*results)
 
 
 def fast(
@@ -633,6 +669,10 @@
     hbm = pl.BlockSpec(memory_space=pl.ANY)
     dma = lambda *shape: pltpu.SemaphoreType.DMA(shape)
     scratch = [
+        pltpu.VMEM((2048, 256), BF16),
+        pltpu.VMEM((2048, 256), BF16),
+        pltpu.VMEM((2048, 256), BF16),
+        pltpu.VMEM((256, 2048), BF16),
         pltpu.VMEM((256, 256), BF16),
         pltpu.VMEM((3, 256, 2048), BF16),
         pltpu.VMEM((3, 256, 2048), BF16),
@@ -657,7 +697,7 @@
         pltpu.VMEM((3, 8, 256), F32),
         dma(2, 6),
         dma(2, 9),
-        dma(10),
+        dma(14),
     ]
     for n in (2, 1, 1):
         scratch += [dma(2, count * n) for count in (3, 3, 2, 4, 8)]
@@ -679,7 +719,7 @@
         kernel,
         out_shape=tuple(jax.ShapeDtypeStruct(shape, BF16) for shape in shapes),
         in_specs=[smem, smem, vmem, vmem, vmem, hbm, hbm, hbm, hbm],
-        out_specs=(vmem,) * 7,
+        out_specs=(vmem,) * 3 + (hbm,) * 4,
         scratch_shapes=scratch,
         compiler_params=pltpu.CompilerParams(
             collective_id=0, has_side_effects=True, vmem_limit_bytes=58 * 2**20
@@ -689,6 +729,7 @@
         enc_lengths, dec_lengths, dec_input[0], enc_output[0], cotangent[0],
         query_weight, key_weight, value_weight, output_weight,
     )
+    results = write_out(results)
     return tuple(out[None] for out in results[:3]) + tuple(results[3:])
 
 

time: 144 us -> 266 us (1.85)
  Pallas kernels: 132 us -> 264 us
  local copies, waits for them, and re-layouts: 9.74 us -> 0 us
    pallas_call x0 -> x1, Pallas kernels: none -> 140 us  [write_out(): pl.pallas_call(write_kernel, out_shape=tuple((jax.ShapeDtypeStruct(r.shap...]
    unnamed x17 -> x0, local copies, waits for them, and re-layouts: 9.74 us -> none
    pallas_call x1, Pallas kernels: 132 us -> 124 us  [fast(): pl.pallas_call(kernel, out_shape=tuple((jax.ShapeDtypeStruct(shape, BF16)...]
where the time goes in v4:
time: 266 us
  Pallas kernels  264 us (99%)
    pallas_call x1, Pallas kernels, write_out(): pl.pallas_call(write_kernel, out_shape=tuple((jax.ShapeDtypeStruct(r.shap...  140 us
    pallas_call x1, Pallas kernels, fast(): pl.pallas_call(kernel, out_shape=tuple((jax.ShapeDtypeStruct(shape, BF16)...  124 us

profile of v4, /device:TPU:14, one launch (start us, length us, event | category | flops | bytes accessed | tf_op | source)
XLA Modules:
  0.0 266.2 jit_solution(10543338942707919417)
XLA Ops:
  1.9 124.2 %cross_attention.1 = (bf16[256,256]{1,0:T(8,128)(2,1)}, bf16[256,256]{1,0:T(8,128)(2,1)}, bf16[16,4096]{1,0:T(8,128)(2,1)}, bf16[2048,256]{1,0:T(8,128)(2,1)}, b...) custom-call(s32[1]{0:T(128)S(6)} %copy.16.enc_len, s32[1]{0:T(128)S(6)} %copy.17.dec_len, ...), custom_call_target="tpu_custom_call" | custom-call | tf_op jit(solution)/shard_map/cross_attention/pallas_call | solution.py:718
  126.1 140.1 %write_out.1 = (bf16[256,256]{1,0:T(8,128)(2,1)}, bf16[256,256]{1,0:T(8,128)(2,1)}, bf16[16,4096]{1,0:T(8,128)(2,1)}, bf16[2048,256]{1,0:T(8,128)(2,1)}, bf16[20...) custom-call(bf16[256,256]{1,0:T(8,128)(2,1)} %get-tuple-element.21.refs_0_, ...), custom_call_target="tpu_custom_call" | custom-call | tf_op jit(solution)/shard_map/write_out/pallas_call | solution.py:645

commit v5 on v4

--- a/solution.py
+++ b/solution.py
@@ -1,3 +1,5 @@
+import functools
+
 import functools
 
 import jax
@@ -630,24 +632,28 @@
     sends.finish()
 
 
-def write_kernel(*refs):
-    n = (len(refs) - 1) // 2
-    sems = refs[-1]
-    copies = [pltpu.make_async_copy(refs[i], refs[n + i], sems.at[i]) for i in range(n)]
-    for copy in copies:
+def write_kernel(n, *refs):
+    sources, outs, held, sems = refs[:n], refs[n : 2 * n], refs[2 * n : 3 * n], refs[3 * n]
+    reads = [pltpu.make_async_copy(sources[i], held[i], sems.at[i]) for i in range(n)]
+    writes = [pltpu.make_async_copy(held[i], outs[i], sems.at[n + i]) for i in range(n)]
+    for copy in reads:
         copy.start()
-    for copy in copies:
+    for read, write in zip(reads, writes):
+        read.wait()
+        write.start()
+    for copy in writes:
         copy.wait()
 
 
 def write_out(results):
     hbm = pl.BlockSpec(memory_space=pl.ANY)
     return pl.pallas_call(
-        write_kernel,
+        functools.partial(write_kernel, len(results)),
         out_shape=tuple(jax.ShapeDtypeStruct(r.shape, r.dtype) for r in results),
         in_specs=[hbm] * len(results),
         out_specs=(hbm,) * len(results),
-        scratch_shapes=[pltpu.SemaphoreType.DMA((len(results),))],
+        scratch_shapes=[pltpu.VMEM(r.shape, r.dtype) for r in results]
+        + [pltpu.SemaphoreType.DMA((2 * len(results),))],
         compiler_params=pltpu.CompilerParams(vmem_limit_bytes=60 * 2**20),
         name="write_out",
     )(*results)

time: 266 us -> 130 us (0.49)
  Pallas kernels: 264 us -> 128 us
    pallas_call x1, Pallas kernels: 140 us -> 3.97 us  [write_out(): pl.pallas_call(functools.partial(write_kernel, len(results)), out_shape=t...]
where the time goes in v5:
time: 130 us
  Pallas kernels  128 us (98%)
  between operations  1.93 us (1%)
    pallas_call x1, Pallas kernels, fast(): pl.pallas_call(kernel, out_shape=tuple((jax.ShapeDtypeStruct(shape, BF16)...  124 us
    pallas_call x1, Pallas kernels, write_out(): pl.pallas_call(functools.partial(write_kernel, len(results)), out_shape=t...  3.97 us

profile of v5, /device:TPU:14, one launch (start us, length us, event | category | flops | bytes accessed | tf_op | source)
XLA Modules:
  0.0 130.1 jit_solution(11296945716208131516)
XLA Ops:
  1.9 124.2 %cross_attention.1 = (bf16[256,256]{1,0:T(8,128)(2,1)}, bf16[256,256]{1,0:T(8,128)(2,1)}, bf16[16,4096]{1,0:T(8,128)(2,1)}, bf16[2048,256]{1,0:T(8,128)(2,1)}, b...) custom-call(s32[1]{0:T(128)S(6)} %copy.16.enc_len, s32[1]{0:T(128)S(6)} %copy.17.dec_len, ...), custom_call_target="tpu_custom_call" | custom-call | tf_op jit(solution)/shard_map/cross_attention/pallas_call | solution.py:724
  126.1 4.0 %write_out.1 = (bf16[256,256]{1,0:T(8,128)(2,1)}, bf16[256,256]{1,0:T(8,128)(2,1)}, bf16[16,4096]{1,0:T(8,128)(2,1)}, bf16[2048,256]{1,0:T(8,128)(2,1)}, bf16[20...) custom-call(bf16[256,256]{1,0:T(8,128)(2,1)} %get-tuple-element.21.refs_0_, ...), custom_call_target="tpu_custom_call" | custom-call | tf_op jit(solution)/shard_map/write_out/pallas_call | solution.py:650

commit v6 on v5

--- a/solution.py
+++ b/solution.py
@@ -559,6 +559,15 @@
     across_core(ro, 1 - y)
     across_x(ro, y)
     across_x(ro, 1 - y)
+
+    @pl.loop(0, 4)
+    def _(i):
+        cols = chunk(i, 512)
+        total = matmul(grads[ATT, 0], gc[0, :, cols], BY_TOKENS)
+        total += matmul(grads[ATT, 1], gc[1, :, cols], BY_TOKENS)
+        output_grad[:, cols] = total.astype(BF16)
+
+    emit(ATT, output_grad)
 
     attended_grad = projected(3)
     probs_grad = matmul(attended_grad, valued, BY_ROWS)
@@ -600,19 +609,10 @@
             None, stat_sum.at[2], stat_got.at[2 + step], stat_sems, 2 + step, line_peer(*here, step)
         )
     along_z(rn)
-    weight_part(value_grad, ge, VG)
     across_y(re, True)
     across_y(re, False)
     along_z(re)
-
-    @pl.loop(0, 4)
-    def _(i):
-        cols = chunk(i, 512)
-        total = matmul(grads[ATT, 0], gc[0, :, cols], BY_TOKENS)
-        total += matmul(grads[ATT, 1], gc[1, :, cols], BY_TOKENS)
-        output_grad[:, cols] = total.astype(BF16)
-
-    emit(ATT, output_grad)
+    weight_part(value_grad, ge, VG)
 
     layer_out[...] = (dec[...].astype(F32) + summed(ro)).astype(BF16)
     total = stat_sum[2]

time: 130 us -> 130 us (level)
  no operation moved by 1% of the time
where the time goes in v6:
time: 130 us
  Pallas kernels  128 us (98%)
  between operations  1.93 us (1%)
    pallas_call x1, Pallas kernels, fast(): pl.pallas_call(kernel, out_shape=tuple((jax.ShapeDtypeStruct(shape, BF16)...  124 us
    pallas_call x1, Pallas kernels, write_out(): pl.pallas_call(functools.partial(write_kernel, len(results)), out_shape=t...  3.97 us

profile of v6, /device:TPU:14, one launch (start us, length us, event | category | flops | bytes accessed | tf_op | source)
XLA Modules:
  0.0 130.0 jit_solution(557185148277554102)
XLA Ops:
  1.9 124.1 %cross_attention.1 = (bf16[256,256]{1,0:T(8,128)(2,1)}, bf16[256,256]{1,0:T(8,128)(2,1)}, bf16[16,4096]{1,0:T(8,128)(2,1)}, bf16[2048,256]{1,0:T(8,128)(2,1)}, b...) custom-call(s32[1]{0:T(128)S(6)} %copy.16.enc_len, s32[1]{0:T(128)S(6)} %copy.17.dec_len, ...), custom_call_target="tpu_custom_call" | custom-call | tf_op jit(solution)/shard_map/cross_attention/pallas_call | solution.py:724
  126.1 4.0 %write_out.1 = (bf16[256,256]{1,0:T(8,128)(2,1)}, bf16[256,256]{1,0:T(8,128)(2,1)}, bf16[16,4096]{1,0:T(8,128)(2,1)}, bf16[2048,256]{1,0:T(8,128)(2,1)}, bf16[20...) custom-call(bf16[256,256]{1,0:T(8,128)(2,1)} %get-tuple-element.21.refs_0_, ...), custom_call_target="tpu_custom_call" | custom-call | tf_op jit(solution)/shard_map/write_out/pallas_call | solution.py:650
